TPU v7x, 256 devices: a whole 4x4x8 slice. The times are simulated.
256 devices in a mesh: dp: 8 (over z), expert: 16 (over x, y), opt: 2 (over core).
Axes of the slice: x: 4, y: 4, z: 8, core: 2. Of those that a mesh axis runs over, the one named last changes fastest.
Arguments:
- tokens: bfloat16 [65536, 4096], P(('dp', 'expert', 'opt')), may hold values from -6 to 6
- routing: int32 [65536, 8], P(('dp', 'expert', 'opt')), may hold values from 0 to 127, all different within a row; in each aligned block of 256 rows (0 to 255, 256 to 511, ...) at most 32 rows name the same one
- grad_gate: bfloat16 [8, 16, 2, 512, 1536], P('dp', 'expert', 'opt'), may hold values from -0.0625 to 0.0625
- touched_mask: int32 [16, 32, 12], P('expert', ('dp', 'opt')), may hold values 0 or 1
- params: float32 [16, 4096, 1536], P('expert', ('dp', 'opt')), may hold values from -3 to 3
- moment_one: float32 [16, 4096, 1536], P('expert', ('dp', 'opt')), may hold values from -2 to 2
- moment_two: float32 [16, 4096, 1536], P('expert', ('dp', 'opt')), may hold values from 0.01 to 1
Outputs:
- new_params: float32 [16, 4096, 1536], P('expert', ('dp', 'opt'))
- new_moment_one: float32 [16, 4096, 1536], P('expert', ('dp', 'opt'))
- new_moment_two: float32 [16, 4096, 1536], P('expert', ('dp', 'opt'))
Inputs may be any that keep to these rules, and one draw needn't show every extreme that they name: `routing`: among the 2048 entries of one device no expert is named more than 32 times, a bound that some block reaches; a token's 8 experts differ.
All inputs are finite; a program needn't handle non-finite values. No bound on the sum of `touched_mask` on one device may be relied on, other than what follows from the above.
Results may differ from a plain program's by a relative error of at most 0.0006.
Values may be sent and summed in bfloat16 or wider, within the bound.
No kernel may reach another device: no remote copies, remote signals or barrier semaphores. Data moves between devices by JAX's collectives and lax.ppermute only.
A program may use at most 128 MiB of HBM per device.

v0:
```python
import jax
import jax.numpy as jnp
from jax import lax
from jax.sharding import PartitionSpec as P

TILE = 128


def expand_tiles(tiles):
    return jnp.repeat(jnp.repeat(tiles, TILE, axis=0), TILE, axis=1)


def per_device(tokens, routing, grad_gate, touched_mask, params, moment_one, moment_two):
    n_expert = lax.axis_size("expert")
    width = tokens.shape[1]
    hidden = grad_gate.shape[4]
    capacity = grad_gate.shape[3] // n_expert
    entries = routing.reshape(-1)
    onehot = (entries[:, None] == jnp.arange(n_expert, dtype=jnp.int32)).astype(jnp.int32)
    before = jnp.cumsum(onehot, axis=0) - onehot
    slot = jnp.sum(before * onehot, axis=1)
    target = jnp.where(entries < n_expert, entries * capacity + slot, n_expert * capacity)
    repeated = jnp.repeat(tokens, routing.shape[1], axis=0)
    outgoing = (
        jnp.zeros((n_expert * capacity, width), jnp.bfloat16).at[target].set(repeated, mode="drop")
    )
    arrived = lax.all_to_all(
        outgoing.reshape(n_expert, capacity, width),
        "expert",
        split_axis=0,
        concat_axis=0,
        tiled=True,
    )
    arrived = arrived.reshape(n_expert * capacity, width)
    slot_grads = grad_gate.reshape(-1, hidden)
    part = lax.dot_general(
        arrived, slot_grads, (((0,), (0,)), ((), ())), preferred_element_type=jnp.float32
    )
    grad = lax.psum_scatter(
        lax.optimization_barrier(part.astype(jnp.bfloat16)).astype(jnp.float32),
        ("dp", "opt"),
        scatter_dimension=0,
        tiled=True,
    )
    live = expand_tiles(touched_mask[0]) > 0
    weight = params[0]
    first = moment_one[0]
    second = moment_two[0]
    first_new = 0.9 * first + 0.1 * grad
    second_new = 0.95 * second + 0.05 * grad * grad
    step = first_new / (1.0 - 0.9**10) / (jnp.sqrt(second_new / (1.0 - 0.95**10)) + 1e-08)
    weight_new = weight - 0.01 * (step + 0.1 * weight)
    out_weight = jnp.where(live, weight_new, weight)[None]
    out_first = jnp.where(live, first_new, first)[None]
    out_second = jnp.where(live, second_new, second)[None]
    return (out_weight, out_first, out_second)


def solution(mesh):
    placed = (
        P(("dp", "expert", "opt"), None),
        P(("dp", "expert", "opt"), None),
        P("dp", "expert", "opt", None, None),
        P("expert", ("dp", "opt"), None),
        P("expert", ("dp", "opt"), None),
        P("expert", ("dp", "opt"), None),
        P("expert", ("dp", "opt"), None),
    )
    return jax.shard_map(
        per_device,
        mesh=mesh,
        in_specs=placed,
        out_specs=(
            P("expert", ("dp", "opt"), None),
            P("expert", ("dp", "opt"), None),
            P("expert", ("dp", "opt"), None),
        ),
        check_vma=False,
    )
```

profile of v0, /device:TPU:2, one launch (start us, length us, event | category | flops | bytes accessed | tf_op | source)
XLA Modules:
  0.0 271.2 jit_solution(16274410587809872256)
XLA Ops:
  7.2 0.0 copy-start
  7.2 0.0 reduce-scatter.2.cloned.1.call-start
  7.2 1.0 copy.21
  8.2 0.1 eq.29
  8.3 0.1 eq.25
  8.4 0.7 broadcast_multiply_fusion
  9.1 0.7 broadcast_compare_fusion
  9.8 4.5 %reduce-window.6 = s32[16,16,128]{2,1,0:T(8,128)S(1)} reduce-window(s32[16,16,128]{2,1,0:T(8,128)S(1)} %fusion.15, s32[]{:T(128)} %constant.13.clone.1), window={size=1x1x128 pad=0_0x0_0x127_0}, to_apply=%region_0.0 | reduce-window | flops 4161536 | bytes 262148 | tf_op jit(solution)/shard_map/reduce-window
  14.4 0.4 slice_reduce_fusion
  14.8 0.2 reduce-window.9
  15.0 0.1 broadcast_add_fusion
  15.1 0.1 copy.20
  15.2 0.1 mul.56
  15.3 0.2 copy.19
  15.5 0.1 lt.31
  15.6 0.1 fusion.14
  15.8 0.0 copy-done
  15.8 24.0 %scatter_custom_fusion = bf16[512,4096]{1,0:T(8,128)(2,1)} fusion(s32[2048]{0:T(1024)S(1)} %bitcast.83, bf16[256,4096]{1,0:T(8,128)(2,1)S(1)} %copy-done, bf16[]{:T(256)} %constant.15.clone.1), kind=kCustom, calls=%fused_computation.1 | custom fusion | bytes 6291458 | tf_op jit(solution)/shard_map/scatter | solution.py:25
  39.8 0.0 copy-start.1
  39.8 56.8 %all_to_all.5 = bf16[16,32,4096]{2,1,0:T(8,128)(2,1)S(1)} all-to-all(bf16[16,32,4096]{2,1,0:T(8,128)(2,1)} %bitcast.75), channel_id=1, replica_groups=mesh['dp'=8,'expert'=16,'opt'=2] {'expert'}, dimensions={0} | all-to-all | bytes 8388608 | tf_op jit(solution)/shard_map/all_to_all | solution.py:27
  96.6 0.0 copy-done.1
  96.6 7.0 %convolution_convert_fusion = bf16[4096,1536]{1,0:T(8,128)(2,1)S(1)} fusion(bf16[512,4096]{1,0:T(8,128)(2,1)S(1)} %bitcast.76, bf16[1,1,1,512,1536]{4,3,2,1,0:T(8,128)(2,1)S(1)} %copy-done.1), kind=kOutput, calls=%fused_computation.3 | convolution fusion | flops 6448742400 | bytes 18350080 | tf_op jit(solution)/shard_map/dot_general | solution.py:36
  103.7 9.7 %convert_element_type.16 = f32[4096,1536]{1,0:T(8,128)} convert(bf16[4096,1536]{1,0:T(8,128)(2,1)S(1)} %convolution_convert_fusion) | non-fusion elementwise | flops 6291456 | bytes 37748736 | tf_op jit(solution)/shard_map/convert_element_type | solution.py:40
  113.3 0.0 copy-start.2
  113.3 0.0 reduce-scatter.2.cloned.1.call-update
  113.4 0.7 copy-done.2
  114.0 0.1 copy.18
  114.1 0.1 broadcast_bitcast_fusion
  114.2 0.1 broadcast_in_dim.28
  114.4 0.6 copy.23
  114.9 142.7 %reduce-scatter.2.cloned.1.call-done = f32[256,1536]{1,0:T(8,128)} async-done(((f32[4096,1536]{1,0:T(8,128)}), f32[256,1536]{1,0:T(8,128)}) %reduce-scatter.2.cloned.1.call-update) | async-done | bytes 1572880 | tf_op jit(solution)/shard_map/reduce_scatter | solution.py:39
  257.6 6.8 %fusion.6 = (f32[1,256,1536]{2,1,0:T(8,128)}, f32[1,256,1536]{2,1,0:T(8,128)}, f32[1,256,1536]{2,1,0:T(8,128)}) fusion(pred[256,1536]{1,0:T(8,128)(4,1)S(1)} %copy.23, f32[1,256,1536]{2,1,0:T(8,128)} %param.13, f32[256,1536]{1,0:T(8,128)} %reduce-scatter.2.cloned.1.call-done, f32[1,256,1536]{2,1,0:T(8,128)} %param.12, f32[1,256,1536]{2,1,0:T(8,128)} %param.11), kind=kLoop, calls=%fused_computation.12 | loop fusion | flops 7077888 | bytes 11403264 | tf_op jit(solution)/shard_map/broadcast_in_dim | solution.py:55
  (5 shorter events, 0.1 us)
Async XLA Ops:
  7.2 8.6 %copy-start = (bf16[256,4096]{1,0:T(8,128)(2,1)S(1)}, bf16[256,4096]{1,0:T(8,128)(2,1)}, u32[]{:S(2)}) copy-start(bf16[256,4096]{1,0:T(8,128)(2,1)} %param.7) | copy-start | bytes 6291460
  7.2 250.4 %reduce-scatter.2.cloned.1.call-start = ((), (), s32[]{:S(2)}) async-start(), calls=%async_computation.2 | async-start | bytes 26738688 | tf_op jit(solution)/shard_map/reduce_scatter | solution.py:39
  39.8 56.9 %copy-start.1 = (bf16[1,1,1,512,1536]{4,3,2,1,0:T(8,128)(2,1)S(1)}, bf16[1,1,1,512,1536]{4,3,2,1,0:T(8,128)(2,1)}, u32[]{:S(2)}) copy-start(bf16[1,1,1,512,1536]{4,3,2,1,0:T(8,128)(2,1)} %param.9) | copy-start | bytes 4718596
  113.3 0.7 copy-start.2
Sparse Core Ops, SparseCore 0:
  113.5 144.0 reduce-scatter.1
where the time goes:
time: 272 us; the launch traced here: 271 us
  waiting for transfers between devices  143 us (53%)
  blocking collectives  56.8 us (21%)
  local copies, waits for them, and re-layouts  27.7 us (10%)
  other arithmetic  22.7 us (8%)
  between operations  14.2 us (5%)
  matrix products  7.03 us (3%)
    reduce_scatter x1, waiting for transfers between devices, per_device(): lax.psum_scatter(lax.optimization_barrier(part.astype(jnp.bfloat16)).asty...  143 us
    all_to_all x1, blocking collectives, per_device(): lax.all_to_all(outgoing.reshape(n_expert, capacity, width), 'expert', spl...  56.8 us
    scatter x1, local copies, waits for them, and re-layouts, per_device(): jnp.zeros((n_expert * capacity, width), jnp.bfloat16).at[target]  24 us
    convert_element_type x1, other arithmetic, per_device(): lax.optimization_barrier(part.astype(jnp.bfloat16)).astype(jnp.float32)  9.67 us
    dot_general x1, matrix products, per_device(): lax.dot_general(arrived, slot_grads, (((0,), (0,)), ((), ())), preferred_...  7.03 us
    broadcast_in_dim x1, other arithmetic, per_device(): out_second = jnp.where(live, second_new, second)[None]  6.75 us
  transfers between devices with their start and end apart: 1, of which 1 were waited for; matrix products, arithmetic and copies ran while one was open for 0% of the time, Pallas kernels for 0%

commit v1 on v0

v1 whole, which is shorter than its diff:
```python
import jax
import jax.numpy as jnp
from jax import lax
from jax.experimental import pallas as pl
from jax.experimental.pallas import tpu as pltpu
from jax.sharding import PartitionSpec as P

TILE = 128
CAP = 32
EXPERTS = 16
N_DP = 8
HALF = 256
WIRE_SCALE = 16.0


def dispatch_kernel(blocks_ref, routes_ref, *refs):
    *token_refs, out_ref, pick_ref = refs
    count = token_refs[0].shape[0]

    @pl.when(pl.program_id(0) == 0)
    def _():
        expert = lax.broadcasted_iota(jnp.int32, (EXPERTS, count), 0)
        named = routes_ref[0:1, :] == expert
        for k in range(1, routes_ref.shape[0]):
            named = jnp.logical_or(named, routes_ref[k : k + 1, :] == expert)
        named = named.astype(jnp.float32)
        row = lax.broadcasted_iota(jnp.int32, (count, count), 0)
        column = lax.broadcasted_iota(jnp.int32, (count, count), 1)
        earlier = (row < column).astype(jnp.bfloat16)
        before = jnp.dot(named.astype(jnp.bfloat16), earlier, preferred_element_type=jnp.float32)
        place = jnp.where(named > 0, before, -1.0).astype(jnp.int32)
        slot = lax.broadcasted_iota(jnp.int32, (CAP, count), 0)
        for e in range(EXPERTS):
            hit = place[e : e + 1, :] == slot
            pick_ref[e * CAP : (e + 1) * CAP, :] = hit.astype(jnp.float32).astype(jnp.bfloat16)

    for j, token_ref in enumerate(token_refs):
        out_ref[:, j * HALF : (j + 1) * HALF] = jnp.dot(
            pick_ref[...], token_ref[...], preferred_element_type=jnp.float32
        ).astype(out_ref.dtype)


def dispatch(blocks, routes, tokens):
    rows = EXPERTS * CAP
    count = tokens.shape[0]
    halves = blocks.shape[0] // 2

    def block(j):
        return pl.BlockSpec((count, HALF), lambda i, blocks: (0, blocks[i * halves + j]))

    return pl.pallas_call(
        dispatch_kernel,
        grid_spec=pltpu.PrefetchScalarGridSpec(
            num_scalar_prefetch=1,
            grid=(2,),
            in_specs=[pl.BlockSpec(routes.shape, lambda i, blocks: (0, 0))]
            + [block(j) for j in range(halves)],
            out_specs=pl.BlockSpec((rows, halves * HALF), lambda i, blocks: (i, 0)),
            scratch_shapes=[pltpu.VMEM((rows, count), jnp.bfloat16)],
        ),
        out_shape=jax.ShapeDtypeStruct((2 * rows, halves * HALF), jnp.bfloat16),
        compiler_params=pltpu.CompilerParams(vmem_limit_bytes=60 << 20),
        cost_estimate=pl.CostEstimate(
            flops=2 * 2 * rows * halves * HALF * count,
            bytes_accessed=2 * halves * HALF * (count + rows) * 2,
            transcendentals=0,
        ),
        name="dispatch",
    )(blocks, routes, *([tokens] * halves))


def product_kernel(core_ref, *refs):
    *x_refs, g_mine, g_other, out_ref = refs
    count = len(x_refs) // 2

    def part(x, g):
        contract = (((0,), (0,)), ((), ()))
        p = lax.dot_general(x, g, contract, preferred_element_type=jnp.float32)
        return p.astype(jnp.bfloat16).astype(jnp.float32)

    for j in range(count):
        out_ref[j * HALF : (j + 1) * HALF, :] = (
            part(x_refs[j][0], g_mine[...]) + part(x_refs[count + j][0], g_other[...])
        ) * WIRE_SCALE


def product(core, arrived, mine, other, blocks):
    slots, hidden = mine.shape
    tile = 768
    rows = len(blocks) * HALF

    def of_mine(j):
        return pl.BlockSpec((1, slots, HALF), lambda n, core: (core[0], 0, j))

    def of_other(j):
        return pl.BlockSpec((1, slots, HALF), lambda n, core: (1 - core[0], 0, j))

    return pl.pallas_call(
        product_kernel,
        grid_spec=pltpu.PrefetchScalarGridSpec(
            num_scalar_prefetch=1,
            grid=(hidden // tile,),
            in_specs=[of_mine(j) for j in blocks]
            + [of_other(j) for j in blocks]
            + [
                pl.BlockSpec((slots, tile), lambda n, core: (0, n)),
                pl.BlockSpec((slots, tile), lambda n, core: (0, n)),
            ],
            out_specs=pl.BlockSpec((rows, tile), lambda n, core: (0, n)),
        ),
        out_shape=jax.ShapeDtypeStruct((rows, hidden), jnp.float32),
        compiler_params=pltpu.CompilerParams(vmem_limit_bytes=24 << 20),
        cost_estimate=pl.CostEstimate(
            flops=2 * 2 * slots * rows * hidden,
            bytes_accessed=4 * slots * (rows + hidden) + 4 * rows * hidden,
            transcendentals=0,
        ),
        name="product",
    )(core, *([arrived] * (2 * len(blocks))), mine, other)


def after(x, *others):
    return lax.optimization_barrier((x,) + others)[0]


def per_device(tokens, routing, grad_gate, touched_mask, params, moment_one, moment_two):
    r = lax.axis_index("dp")
    core = lax.axis_index("opt").astype(jnp.int32).reshape(1)
    slots = EXPERTS * CAP
    routes = routing.T
    mine = grad_gate[0, 0, 0]
    other = lax.ppermute(mine, "opt", [(0, 1), (1, 0)])

    ahead = [(i * 2 + o, ((i + (1 - 2 * o)) % N_DP) * 2 + o) for i in range(N_DP) for o in range(2)]
    across = [(i * 2 + o, ((i + (1 - 2 * o)) % N_DP) * 2 + 1 - o) for i in range(N_DP) for o in range(2)]

    def gathered(pairs):
        up = [2 * ((r + k) % N_DP) + other_core for k, other_core in pairs]
        down = [2 * ((r - k) % N_DP) + 1 - other_core for k, other_core in pairs]
        return dispatch(jnp.stack(up + down).astype(jnp.int32), routes, tokens)

    def exchange(sent):
        sent = sent.reshape(2 * EXPERTS, CAP, -1)
        return lax.all_to_all(sent, ("opt", "expert"), 0, 0, tiled=True).reshape(2, slots, -1)

    def totals(arrived, blocks):
        out = product(core, arrived, mine, other, blocks)
        return [out[j * HALF : (j + 1) * HALF] for j in range(len(blocks))]

    def plus(x, received):
        return x + received.astype(jnp.float32)

    def pack(x):
        return x.astype(jnp.float16)

    def shift(x, pairs):
        return lax.ppermute(x, ("dp", "opt"), pairs)

    sent = gathered([(4, 0), (3, 1), (3, 0), (2, 1)])
    arrived = exchange(sent)
    sent = after(gathered([(2, 0), (1, 1), (1, 0), (0, 0)]), sent)
    arrived, sent = lax.optimization_barrier((arrived, sent))
    (own,) = totals(arrived, [0])
    near_out = pack(own)
    near = shift(near_out, ahead)
    late = exchange(after(sent, near_out))
    three_b, three_a, two_b = totals(after(arrived, near_out), [1, 2, 3])
    far_out = pack(three_b)
    far = shift(far_out, ahead)
    near_out = pack(plus(three_a, after(near, far_out)))
    near = shift(near_out, ahead)
    far_out = pack(plus(two_b, after(far, near_out)))
    far = shift(far_out, ahead)
    (two_a,) = totals(late, [0])
    near_out = pack(plus(two_a, after(near, far_out)))
    near = shift(near_out, ahead)
    one_b, one_a, own = totals(after(late, near_out), [1, 2, 3])
    far_out = pack(plus(one_b, after(far, near_out)))
    far = shift(far_out, across)
    near_out = pack(plus(one_a, after(near, far_out)))
    near = shift(near_out, ahead)
    grad = plus(plus(own, far), near) * (1.0 / WIRE_SCALE)

    live = jnp.repeat(jnp.repeat(touched_mask[0], TILE, axis=0), TILE, axis=1) > 0
    weight = params[0]
    first = moment_one[0]
    second = moment_two[0]
    first_new = 0.9 * first + 0.1 * grad
    second_new = 0.95 * second + 0.05 * grad * grad
    scaled_first = first_new * (1.0 / (1.0 - 0.9**10))
    scaled_second = second_new * (1.0 / (1.0 - 0.95**10))
    step = scaled_first / (jnp.sqrt(scaled_second) + 1e-08)
    weight_new = weight - 0.01 * (step + 0.1 * weight)
    out_weight = jnp.where(live, weight_new, weight)[None]
    out_first = jnp.where(live, first_new, first)[None]
    out_second = jnp.where(live, second_new, second)[None]
    return (out_weight, out_first, out_second)


def solution(mesh):
    rows = P(("dp", "expert", "opt"), None)
    state = P("expert", ("dp", "opt"), None)
    return jax.shard_map(
        per_device,
        mesh=mesh,
        in_specs=(rows, rows, P("dp", "expert", "opt", None, None), state, state, state, state),
        out_specs=(state, state, state),
        check_vma=False,
    )
```

time: 272 us -> 127 us (0.47)
  waiting for transfers between devices: 143 us -> 65 us
  blocking collectives: 56.8 us -> 0 us
  Pallas kernels: 0 us -> 22.5 us
  local copies, waits for them, and re-layouts: 27.7 us -> 6.74 us
  starting transfers between devices: 0.04 us -> 19.2 us
  between operations: 14.2 us -> 0.88 us
  other arithmetic: 22.7 us -> 12.1 us
  matrix products: 7.03 us -> 0 us
    reduce_scatter x1 -> x0, waiting for transfers between devices: 143 us -> none  [per_device(): lax.psum_scatter(lax.optimization_barrier(part.astype(jnp.bfloat16)).asty...]
    all_to_all x1 -> x0, blocking collectives: 56.8 us -> none  [per_device(): lax.all_to_all(outgoing.reshape(n_expert, capacity, width), 'expert', spl...]
    ppermute x0 -> x8, waiting for transfers between devices: none -> 39.1 us  [the longest x7 39.1 us: shift(): return lax.ppermute(x, ('dp', 'opt'), pairs)]
    all_to_all x0 -> x2, waiting for transfers between devices: none -> 25.9 us  [exchange(): lax.all_to_all(sent, ('opt', 'expert'), 0, 0, tiled=True)]
    scatter x1 -> x0, local copies, waits for them, and re-layouts: 24 us -> none  [per_device(): jnp.zeros((n_expert * capacity, width), jnp.bfloat16).at[target]]
    pallas_call x0 -> x6, Pallas kernels: none -> 22.5 us  [the longest x4 14.6 us: product(): pl.pallas_call(product_kernel, grid_spec=pltpu.PrefetchScalarGridSpec(num...]
    all_to_all x0 -> x2, starting transfers between devices: none -> 15.5 us  [exchange(): lax.all_to_all(sent, ('opt', 'expert'), 0, 0, tiled=True)]
    dot_general x1 -> x0, matrix products: 7.03 us -> none  [per_device(): lax.dot_general(arrived, slot_grads, (((0,), (0,)), ((), ())), preferred_...]
  transfers between devices with their start and end apart: 1 -> 10, of which waited for: 1 -> 8; matrix products, arithmetic and copies ran while one was open for 0% -> 7% of each run, Pallas kernels for 0% -> 13%
where the time goes in v1:
time: 127 us; the launch traced here: 126 us
  waiting for transfers between devices  65 us (51%)
  Pallas kernels  22.5 us (18%)
  starting transfers between devices  19.2 us (15%)
  other arithmetic  12.1 us (10%)
  local copies, waits for them, and re-layouts  6.74 us (5%)
    ppermute x7, waiting for transfers between devices, shift(): return lax.ppermute(x, ('dp', 'opt'), pairs)  39.1 us
    all_to_all x2, waiting for transfers between devices, exchange(): lax.all_to_all(sent, ('opt', 'expert'), 0, 0, tiled=True)  25.9 us
    all_to_all x2, starting transfers between devices, exchange(): lax.all_to_all(sent, ('opt', 'expert'), 0, 0, tiled=True)  15.5 us
    pallas_call x4, Pallas kernels, product(): pl.pallas_call(product_kernel, grid_spec=pltpu.PrefetchScalarGridSpec(num...  14.6 us
    pallas_call x2, Pallas kernels, dispatch(): pl.pallas_call(dispatch_kernel, grid_spec=pltpu.PrefetchScalarGridSpec(nu...  7.89 us
    broadcast_in_dim x1, other arithmetic, per_device(): out_second = jnp.where(live, second_new, second)[None]  6.52 us
    convert_element_type x6, other arithmetic, pack(): return x.astype(jnp.float16)  5.45 us
    ppermute x7, starting transfers between devices, shift(): return lax.ppermute(x, ('dp', 'opt'), pairs)  3.48 us
  transfers between devices with their start and end apart: 10, of which 8 were waited for; matrix products, arithmetic and copies ran while one was open for 7% of the time, Pallas kernels for 13%

profile of v1, /device:TPU:2, one launch (start us, length us, event | category | flops | bytes accessed | tf_op | source)
XLA Modules:
  0.0 126.5 jit_solution(18407032116934943387)
XLA Ops:
  0.7 0.7 stack.62.blocks_ref
  1.4 3.9 %dispatch.2 = bf16[1024,1024]{1,0:T(8,128)(2,1)} custom-call(s32[8]{0:T(128)} %stack.62.blocks_ref, s32[8,256]{1,0:T(8,128)} %bitcast.85, bf16[256,4096]{1,0:T(8,128)(2,1)} %refs_3_.3, bf16[256,4096]{1,0:T(8,128)(2,1)} %refs_3_.3, bf16[256,4096]{1,0:T(8,128)(2,1)} %refs_3_.3, bf16[256,4096]{1,0:T(8,128)(2,1)} %refs_3_.3), custom_call_target="tpu_custom_call" | custom-call | flops 536870912 | bytes 3145728 | tf_op jit(solution)/shard_map/dispatch/pallas_call | solution.py:51
  5.3 7.6 %all-to-all-start = ((bf16[32,32,1024]{2,1,0:T(8,128)(2,1)}), bf16[32,32,1024]{2,1,0:T(8,128)(2,1)S(1)}, u32[]{:S(2)}, u32[]{:S(2)}) async-start(bf16[32,32,1024]{2,1,0:T(8,128)(2,1)} %bitcast.82), calls=%async_computation | async-start | bytes 4194304 | tf_op jit(solution)/shard_map/all_to_all | solution.py:144
  13.0 0.2 collective-permute-start
  13.2 0.6 stack.71.blocks_ref
  13.8 4.0 %dispatch.3 = bf16[1024,1024]{1,0:T(8,128)(2,1)} custom-call(s32[8]{0:T(128)} %stack.71.blocks_ref, s32[8,256]{1,0:T(8,128)} %bitcast.86, bf16[256,4096]{1,0:T(8,128)(2,1)} %refs_3_.3, bf16[256,4096]{1,0:T(8,128)(2,1)} %refs_3_.3, bf16[256,4096]{1,0:T(8,128)(2,1)} %refs_3_.3, bf16[256,4096]{1,0:T(8,128)(2,1)} %refs_3_.3), custom_call_target="tpu_custom_call" | custom-call | flops 536870912 | bytes 3145728 | tf_op jit(solution)/shard_map/dispatch/pallas_call | solution.py:51
  17.8 24.4 %all-to-all-done = bf16[32,32,1024]{2,1,0:T(8,128)(2,1)S(1)} async-done(((bf16[32,32,1024]{2,1,0:T(8,128)(2,1)}), bf16[32,32,1024]{2,1,0:T(8,128)(2,1)S(1)}, u32[]{:S(2)}, u32[]{:S(2)}) %all-to-all-start) | async-done | bytes 2097184 | tf_op jit(solution)/shard_map/all_to_all | solution.py:144
  42.2 1.4 %copy-done = bf16[1,1,1,512,1536]{4,3,2,1,0:T(8,128)(2,1)S(1)} copy-done((bf16[1,1,1,512,1536]{4,3,2,1,0:T(8,128)(2,1)S(1)}, bf16[1,1,1,512,1536]{4,3,2,1,0:T(8,128)(2,1)}, u32[]{:S(2)}) %copy-start) | copy-done | bytes 1572888
  43.6 2.6 %product.4 = f32[256,1536]{1,0:T(8,128)S(1)} custom-call(s32[1]{0:T(128)} %bitcast.4.core_ref, bf16[2,512,1024]{2,1,0:T(8,128)(2,1)S(1)} %bitcast.69, bf16[2,512,1024]{2,1,0:T(8,128)(2,1)S(1)} %bitcast.70, bf16[512,1536]{1,0:T(8,128)(2,1)S(1)} %bitcast.78, bf16[512,1536]{1,0:T(8,128)(2,1)} %collective-permute-done.refs_3_.refs_7_), custom_call_target="tpu_custom_call" | custom-call | flops 805306368 | bytes 5242880 | tf_op jit(solution)/shard_map/product/pallas_call | solution.py:98
  46.3 2.0 %collective-permute-start.1 = (f16[256,1536]{1,0:T(8,128)(2,1)S(1)}, f16[256,1536]{1,0:T(8,128)(2,1)}, u32[]{:S(2)}, u32[]{:S(2)}) collective-permute-start(f16[256,1536]{1,0:T(8,128)(2,1)S(1)} %convert_element_type.40), channel_id=1, source_target_pairs={{0,32},{1,225},{32,64},{33,1},{64,96},{65,33},{96,128},{97,65},{12... | collective-permute-start | bytes 2359304 | tf_op jit(solution)/shard_map/ppermute | solution.py:157
  48.3 7.9 %all-to-all-start.1 = ((bf16[32,32,1024]{2,1,0:T(8,128)(2,1)}), bf16[32,32,1024]{2,1,0:T(8,128)(2,1)}, u32[]{:S(2)}, u32[]{:S(2)}) async-start(bf16[32,32,1024]{2,1,0:T(8,128)(2,1)} %bitcast.83), calls=%async_computation.1 | async-start | bytes 4194304 | tf_op jit(solution)/shard_map/all_to_all | solution.py:144
  56.2 1.4 %copy-done.1 = bf16[1,1,1,512,1536]{4,3,2,1,0:T(8,128)(2,1)S(1)} copy-done((bf16[1,1,1,512,1536]{4,3,2,1,0:T(8,128)(2,1)S(1)}, bf16[1,1,1,512,1536]{4,3,2,1,0:T(8,128)(2,1)}, u32[]{:S(2)}) %copy-start.1) | copy-done | bytes 1572888
  57.6 4.5 %product.6 = f32[768,1536]{1,0:T(8,128)S(1)} custom-call(s32[1]{0:T(128)} %bitcast.4.core_ref, bf16[2,512,1024]{2,1,0:T(8,128)(2,1)S(1)} %bitcast.71, bf16[2,512,1024]{2,1,0:T(8,128)(2,1)S(1)} %bitcast.72, bf16[2,512,1024]{2,1,0:T(8,128)(2,1)S(1)} %bitcast.73, bf16[2,512,1024]{2,1,0:T(8,128)(2,1)S(1)} %bitcast.74, bf16[2,512,1024]{2,1,0:T(8,128)(2,1)S(1)} %bitcast.75, ...), custom_call_target="tpu_custom_call" | custom-call | flops 2415919104 | bytes 9437184 | tf_op jit(solution)/shard_map/product/pallas_call | solution.py:98
  62.3 1.3 %fusion.5 = f16[256,1536]{1,0:T(8,128)(2,1)S(1)} fusion(f32[768,1536]{1,0:T(8,128)S(1)} %product.6, f16[256,1536]{1,0:T(8,128)(2,1)} %collective-permute-done.1), kind=kLoop, calls=%fused_computation.12 | loop fusion | flops 1179648 | bytes 3145728 | tf_op jit(solution)/shard_map/convert_element_type | solution.py:154
  63.6 1.0 collective-permute-start.2
  64.7 10.8 %collective-permute-done.3 = f16[256,1536]{1,0:T(8,128)(2,1)S(1)} collective-permute-done((f16[256,1536]{1,0:T(8,128)(2,1)S(1)}, f16[256,1536]{1,0:T(8,128)(2,1)S(1)}, u32[]{:S(2)}, u32[]{:S(2)}) %collective-permute-start.3) | collective-permute-done | bytes 786464 | tf_op jit(solution)/shard_map/ppermute | solution.py:157
  75.4 0.3 fusion.4
  75.8 8.2 %collective-permute-done.2 = f16[256,1536]{1,0:T(8,128)(2,1)} collective-permute-done((f16[256,1536]{1,0:T(8,128)(2,1)S(1)}, f16[256,1536]{1,0:T(8,128)(2,1)}, u32[]{:S(2)}, u32[]{:S(2)}) %collective-permute-start.2) | collective-permute-done | bytes 786464 | tf_op jit(solution)/shard_map/ppermute | solution.py:157
  84.0 1.5 %all-to-all-done.1 = bf16[32,32,1024]{2,1,0:T(8,128)(2,1)} async-done(((bf16[32,32,1024]{2,1,0:T(8,128)(2,1)}), bf16[32,32,1024]{2,1,0:T(8,128)(2,1)}, u32[]{:S(2)}, u32[]{:S(2)}) %all-to-all-start.1) | async-done | bytes 2097184 | tf_op jit(solution)/shard_map/all_to_all | solution.py:144
  85.5 2.7 %product.5 = f32[256,1536]{1,0:T(8,128)S(1)} custom-call(s32[1]{0:T(128)} %bitcast.4.core_ref, bf16[2,512,1024]{2,1,0:T(8,128)(2,1)} %bitcast.26.refs_0_.refs_1_.refs_2_.refs_3_.refs_4_.refs_5_, bf16[2,512,1024]{2,1,0:T(8,128)(2,1)} %bitcast.26.refs_0_.refs_1_.refs_2_.refs_3_.refs_4_.refs_5_, bf16[512,1536]{1,0:T(8,128)(2,1)S(1)} %bitcast.80, ...), custom_call_target="tpu_custom_call" | custom-call | flops 805306368 | bytes 5242880 | tf_op jit(solution)/shard_map/product/pallas_call | solution.py:98
  88.2 1.3 %add_convert_fusion = f16[256,1536]{1,0:T(8,128)(2,1)S(1)} fusion(f32[256,1536]{1,0:T(8,128)S(1)} %product.5, f16[256,1536]{1,0:T(8,128)(2,1)} %collective-permute-done.2), kind=kLoop, calls=%fused_computation.24 | loop fusion | flops 1179648 | bytes 3145728 | tf_op jit(solution)/shard_map/convert_element_type | solution.py:154
  89.5 0.3 collective-permute-start.6
  89.8 2.5 %collective-permute-done.4 = f16[256,1536]{1,0:T(8,128)(2,1)S(1)} collective-permute-done((f16[256,1536]{1,0:T(8,128)(2,1)S(1)}, f16[256,1536]{1,0:T(8,128)(2,1)S(1)}, u32[]{:S(2)}, u32[]{:S(2)}) %collective-permute-start.4) | collective-permute-done | bytes 786464 | tf_op jit(solution)/shard_map/ppermute | solution.py:157
  92.3 4.9 %product.7 = f32[768,1536]{1,0:T(8,128)S(1)} custom-call(s32[1]{0:T(128)} %bitcast.4.core_ref, bf16[2,512,1024]{2,1,0:T(8,128)(2,1)} %bitcast.26.refs_0_.refs_1_.refs_2_.refs_3_.refs_4_.refs_5_, bf16[2,512,1024]{2,1,0:T(8,128)(2,1)} %bitcast.26.refs_0_.refs_1_.refs_2_.refs_3_.refs_4_.refs_5_, ...), custom_call_target="tpu_custom_call" | custom-call | flops 2415919104 | bytes 9437184 | tf_op jit(solution)/shard_map/product/pallas_call | solution.py:98
  97.2 1.3 %fusion.2 = f16[256,1536]{1,0:T(8,128)(2,1)} fusion(f32[768,1536]{1,0:T(8,128)S(1)} %product.7, f16[256,1536]{1,0:T(8,128)(2,1)S(1)} %collective-permute-done.4), kind=kLoop, calls=%fused_computation.5 | loop fusion | flops 1179648 | bytes 3145728 | tf_op jit(solution)/shard_map/convert_element_type | solution.py:154
  98.5 4.5 %collective-permute-done.6 = f16[256,1536]{1,0:T(8,128)(2,1)S(1)} collective-permute-done((f16[256,1536]{1,0:T(8,128)(2,1)S(1)}, f16[256,1536]{1,0:T(8,128)(2,1)S(1)}, u32[]{:S(2)}, u32[]{:S(2)}) %collective-permute-start.6) | collective-permute-done | bytes 786464 | tf_op jit(solution)/shard_map/ppermute | solution.py:157
  103.0 1.2 fusion.1
  104.4 0.9 broadcast_in_dim.16
  105.2 1.5 %copy.15 = pred[256,1536]{1,0:T(8,128)(4,1)S(1)} copy(pred[256,1536]{0,1:T(8,128)(4,1)} %bitcast.84) | data formatting | bytes 786432 | tf_op jit(solution)/shard_map/gt | solution.py:184
  106.8 3.5 %collective-permute-done.5 = f16[256,1536]{1,0:T(8,128)(2,1)} collective-permute-done((f16[256,1536]{1,0:T(8,128)(2,1)}, f16[256,1536]{1,0:T(8,128)(2,1)}, u32[]{:S(2)}, u32[]{:S(2)}) %collective-permute-start.5) | collective-permute-done | bytes 786464 | tf_op jit(solution)/shard_map/ppermute | solution.py:157
  110.2 9.7 %collective-permute-done.7 = f16[256,1536]{1,0:T(8,128)(2,1)} collective-permute-done((f16[256,1536]{1,0:T(8,128)(2,1)}, f16[256,1536]{1,0:T(8,128)(2,1)}, u32[]{:S(2)}, u32[]{:S(2)}) %collective-permute-start.7) | collective-permute-done | bytes 786464 | tf_op jit(solution)/shard_map/ppermute | solution.py:157
  119.9 6.5 %fusion.7 = (f32[1,256,1536]{2,1,0:T(8,128)}, f32[1,256,1536]{2,1,0:T(8,128)}, f32[1,256,1536]{2,1,0:T(8,128)}) fusion(pred[256,1536]{1,0:T(8,128)(4,1)S(1)} %copy.15, f32[1,256,1536]{2,1,0:T(8,128)S(1)} %copy-done.4, f16[256,1536]{1,0:T(8,128)(2,1)} %collective-permute-done.7, f16[256,1536]{1,0:T(8,128)(2,1)} %collective-permute-done.5, ...), kind=kLoop, calls=%fused_computation.16 | loop fusion | flops 9043968 | bytes 12976128 | tf_op jit(solution)/shard_map/broadcast_in_dim | solution.py:196
  (25 shorter events, 0.6 us)
Async XLA Ops:
  5.3 36.9 %all-to-all-start = ((bf16[32,32,1024]{2,1,0:T(8,128)(2,1)}), bf16[32,32,1024]{2,1,0:T(8,128)(2,1)S(1)}, u32[]{:S(2)}, u32[]{:S(2)}) async-start(bf16[32,32,1024]{2,1,0:T(8,128)(2,1)} %bitcast.82), calls=%async_computation | async-start | bytes 4194304 | tf_op jit(solution)/shard_map/all_to_all | solution.py:144
  13.0 29.2 %collective-permute-start = (bf16[512,1536]{1,0:T(8,128)(2,1)}, bf16[512,1536]{1,0:T(8,128)(2,1)}, u32[]{:S(2)}, u32[]{:S(2)}) collective-permute-start(bf16[512,1536]{1,0:T(8,128)(2,1)} %bitcast.77), channel_id=1, source_target_pairs={{0,1},{1,0},{2,3},{3,2},{4,5},{5,4},{6,7},{7,6},{8,9},{9,8},{10,11... | collective-permute-start | bytes 4718600 | tf_op jit(solution)/shard_map/ppermute | solution.py:132
  42.2 1.4 %copy-start = (bf16[1,1,1,512,1536]{4,3,2,1,0:T(8,128)(2,1)S(1)}, bf16[1,1,1,512,1536]{4,3,2,1,0:T(8,128)(2,1)}, u32[]{:S(2)}) copy-start(bf16[1,1,1,512,1536]{4,3,2,1,0:T(8,128)(2,1)} %param.9) | copy-start | bytes 4718596
  46.3 16.0 %collective-permute-start.1 = (f16[256,1536]{1,0:T(8,128)(2,1)S(1)}, f16[256,1536]{1,0:T(8,128)(2,1)}, u32[]{:S(2)}, u32[]{:S(2)}) collective-permute-start(f16[256,1536]{1,0:T(8,128)(2,1)S(1)} %convert_element_type.40), channel_id=1, source_target_pairs={{0,32},{1,225},{32,64},{33,1},{64,96},{65,33},{96,128},{97,65},{12... | collective-permute-start | bytes 2359304 | tf_op jit(solution)/shard_map/ppermute | solution.py:157
  48.3 37.2 %all-to-all-start.1 = ((bf16[32,32,1024]{2,1,0:T(8,128)(2,1)}), bf16[32,32,1024]{2,1,0:T(8,128)(2,1)}, u32[]{:S(2)}, u32[]{:S(2)}) async-start(bf16[32,32,1024]{2,1,0:T(8,128)(2,1)} %bitcast.83), calls=%async_computation.1 | async-start | bytes 4194304 | tf_op jit(solution)/shard_map/all_to_all | solution.py:144
  56.2 1.4 %copy-start.1 = (bf16[1,1,1,512,1536]{4,3,2,1,0:T(8,128)(2,1)S(1)}, bf16[1,1,1,512,1536]{4,3,2,1,0:T(8,128)(2,1)}, u32[]{:S(2)}) copy-start(bf16[1,1,1,512,1536]{4,3,2,1,0:T(8,128)(2,1)} %param.9) | copy-start | bytes 4718596
  62.2 13.3 %collective-permute-start.3 = (f16[256,1536]{1,0:T(8,128)(2,1)S(1)}, f16[256,1536]{1,0:T(8,128)(2,1)S(1)}, u32[]{:S(2)}, u32[]{:S(2)}) collective-permute-start(f16[256,1536]{1,0:T(8,128)(2,1)S(1)} %slice_convert_fusion), channel_id=1, source_target_pairs={{0,32},{1,225},{32,64},{33,1},{64,96},{65,33},{96,128},{97,65},{12... | collective-permute-start | bytes 2359304 | tf_op jit(solution)/shard_map/ppermute | solution.py:157
  63.6 21.9 %copy-start.2 = (bf16[1,1,1,512,1536]{4,3,2,1,0:T(8,128)(2,1)S(1)}, bf16[1,1,1,512,1536]{4,3,2,1,0:T(8,128)(2,1)}, u32[]{:S(2)}) copy-start(bf16[1,1,1,512,1536]{4,3,2,1,0:T(8,128)(2,1)} %param.9) | copy-start | bytes 4718596
  63.6 20.3 %collective-permute-start.2 = (f16[256,1536]{1,0:T(8,128)(2,1)S(1)}, f16[256,1536]{1,0:T(8,128)(2,1)}, u32[]{:S(2)}, u32[]{:S(2)}) collective-permute-start(f16[256,1536]{1,0:T(8,128)(2,1)S(1)} %fusion.5), channel_id=1, source_target_pairs={{0,32},{1,225},{32,64},{33,1},{64,96},{65,33},{96,128},{97,65},{12... | collective-permute-start | bytes 2359304 | tf_op jit(solution)/shard_map/ppermute | solution.py:157
  75.7 16.6 %collective-permute-start.4 = (f16[256,1536]{1,0:T(8,128)(2,1)S(1)}, f16[256,1536]{1,0:T(8,128)(2,1)S(1)}, u32[]{:S(2)}, u32[]{:S(2)}) collective-permute-start(f16[256,1536]{1,0:T(8,128)(2,1)S(1)} %fusion.4), channel_id=1, source_target_pairs={{0,32},{1,225},{32,64},{33,1},{64,96},{65,33},{96,128},{97,65},{12... | collective-permute-start | bytes 2359304 | tf_op jit(solution)/shard_map/ppermute | solution.py:157
  89.5 13.5 %collective-permute-start.6 = (f16[256,1536]{1,0:T(8,128)(2,1)S(1)}, f16[256,1536]{1,0:T(8,128)(2,1)S(1)}, u32[]{:S(2)}, u32[]{:S(2)}) collective-permute-start(f16[256,1536]{1,0:T(8,128)(2,1)S(1)} %add_convert_fusion), channel_id=1, source_target_pairs={{0,32},{1,225},{32,64},{33,1},{64,96},{65,33},{96,128},{97,65},{12... | collective-permute-start | bytes 2359304 | tf_op jit(solution)/shard_map/ppermute | solution.py:157
  97.2 5.8 %copy-start.3 = (f32[768,1536]{1,0:T(8,128)}, f32[768,1536]{1,0:T(8,128)S(1)}, u32[]{:S(2)}) copy-start(f32[768,1536]{1,0:T(8,128)S(1)} %product.7) | copy-start | bytes 14155780
  97.2 6.9 %copy-start.6 = (s32[1,2,12]{2,1,0:T(2,128)S(1)}, s32[1,2,12]{2,1,0:T(2,128)}, u32[]{:S(2)}) copy-start(s32[1,2,12]{2,1,0:T(2,128)} %param.10) | copy-start | bytes 292
  98.5 21.4 %copy-start.4 = (f32[1,256,1536]{2,1,0:T(8,128)S(1)}, f32[1,256,1536]{2,1,0:T(8,128)}, u32[]{:S(2)}) copy-start(f32[1,256,1536]{2,1,0:T(8,128)} %param.13) | copy-start | bytes 4718596
  98.5 21.4 %copy-start.5 = (f32[1,256,1536]{2,1,0:T(8,128)S(1)}, f32[1,256,1536]{2,1,0:T(8,128)}, u32[]{:S(2)}) copy-start(f32[1,256,1536]{2,1,0:T(8,128)} %param.12) | copy-start | bytes 4718596
  98.5 11.7 %collective-permute-start.5 = (f16[256,1536]{1,0:T(8,128)(2,1)}, f16[256,1536]{1,0:T(8,128)(2,1)}, u32[]{:S(2)}, u32[]{:S(2)}) collective-permute-start(f16[256,1536]{1,0:T(8,128)(2,1)} %fusion.2), channel_id=1, source_target_pairs={{0,33},{1,224},{32,65},{33,0},{64,97},{65,32},{96,129},{97,64},{12... | collective-permute-start | bytes 2359304 | tf_op jit(solution)/shard_map/ppermute | solution.py:157
  104.1 15.8 %collective-permute-start.7 = (f16[256,1536]{1,0:T(8,128)(2,1)}, f16[256,1536]{1,0:T(8,128)(2,1)}, u32[]{:S(2)}, u32[]{:S(2)}) collective-permute-start(f16[256,1536]{1,0:T(8,128)(2,1)} %fusion.1), channel_id=1, source_target_pairs={{0,32},{1,225},{32,64},{33,1},{64,96},{65,33},{96,128},{97,65},{12... | collective-permute-start | bytes 2359304 | tf_op jit(solution)/shard_map/ppermute | solution.py:157

commit v2 on v1

v2 whole, which is shorter than its diff:
```python
import functools

import jax
import jax.numpy as jnp
from jax import lax
from jax.experimental import pallas as pl
from jax.experimental.pallas import tpu as pltpu
from jax.sharding import PartitionSpec as P

TILE = 128
CAP = 32
EXPERTS = 16
N_DP = 8
HALF = 256
WIRE_SCALE = 16.0


def picks(routes, count):
    expert = lax.broadcasted_iota(jnp.int32, (EXPERTS, count), 0)
    named = routes[0:1, :] == expert
    for k in range(1, routes.shape[0]):
        named = jnp.logical_or(named, routes[k : k + 1, :] == expert)
    named = named.astype(jnp.float32)
    row = lax.broadcasted_iota(jnp.int32, (count, count), 0)
    column = lax.broadcasted_iota(jnp.int32, (count, count), 1)
    earlier = (row < column).astype(jnp.bfloat16)
    before = jnp.dot(named.astype(jnp.bfloat16), earlier, preferred_element_type=jnp.float32)
    slot_of = jnp.where(named > 0, before, -1.0).astype(jnp.int32)
    slot = lax.broadcasted_iota(jnp.int32, (CAP, count), 0)
    return jnp.concatenate(
        [(slot_of[e : e + 1, :] == slot).astype(jnp.float32) for e in range(EXPERTS)], axis=0
    ).astype(jnp.bfloat16)


def columns_of(r, core, pairs):
    starts = []
    for distance, other in pairs:
        up = 2 * lax.rem(r + distance, N_DP) + other
        down = 2 * lax.rem(r + (N_DP - distance), N_DP) + 1 - other
        block = jnp.where(core == 0, up, down)
        starts.append(pl.multiple_of(block * HALF, HALF))
    return starts


def dispatch_kernel(routes_ref, tokens_ref, out_ref, tokens_in, pick_ref, made, in_sems, out_sems, *, pairs):
    starts = columns_of(lax.axis_index("dp"), 0, pairs) + columns_of(lax.axis_index("dp"), 1, pairs)
    reads = [
        pltpu.make_async_copy(
            tokens_ref.at[:, pl.ds(start, HALF)],
            tokens_in.at[n // len(pairs), :, pl.ds(n % len(pairs) * HALF, HALF)],
            in_sems.at[n],
        )
        for n, start in enumerate(starts)
    ]
    for read in reads:
        read.start()
    pick_ref[...] = picks(routes_ref[...], tokens_ref.shape[0])
    rows = EXPERTS * CAP
    writes = []
    for core in range(2):
        for read in reads[core * len(pairs) : (core + 1) * len(pairs)]:
            read.wait()
        made[core] = jnp.dot(
            pick_ref[...], tokens_in[core], preferred_element_type=jnp.float32
        ).astype(made.dtype)
        write = pltpu.make_async_copy(
            made.at[core], out_ref.at[pl.ds(core * rows, rows), :], out_sems.at[core]
        )
        write.start()
        writes.append(write)
    for write in writes:
        write.wait()


def dispatch(routes, tokens, pairs, limit):
    rows = EXPERTS * CAP
    count = tokens.shape[0]
    blocks = 2 * len(pairs)
    hbm = pl.BlockSpec(memory_space=pltpu.HBM)
    return pl.pallas_call(
        functools.partial(dispatch_kernel, pairs=pairs),
        in_specs=[pl.BlockSpec(memory_space=pltpu.VMEM), hbm],
        out_specs=hbm,
        scratch_shapes=[
            pltpu.VMEM((2, count, len(pairs) * HALF), jnp.bfloat16),
            pltpu.VMEM((rows, count), jnp.bfloat16),
            pltpu.VMEM((2, rows, len(pairs) * HALF), jnp.bfloat16),
            pltpu.SemaphoreType.DMA((blocks,)),
            pltpu.SemaphoreType.DMA((2,)),
        ],
        out_shape=jax.ShapeDtypeStruct((2 * rows, len(pairs) * HALF), jnp.bfloat16),
        compiler_params=pltpu.CompilerParams(vmem_limit_bytes=limit),
        cost_estimate=pl.CostEstimate(
            flops=2 * rows * blocks * HALF * count,
            bytes_accessed=blocks * HALF * (count + rows) * 2,
            transcendentals=0,
        ),
        name="dispatch",
    )(routes, tokens)


def hold_kernel(x_ref, out_ref):
    out_ref[...] = x_ref[...]


def hold(x):
    vmem = pl.BlockSpec(memory_space=pltpu.VMEM)
    return pl.pallas_call(
        hold_kernel,
        in_specs=[vmem],
        out_specs=vmem,
        out_shape=jax.ShapeDtypeStruct(x.shape, x.dtype),
        compiler_params=pltpu.CompilerParams(vmem_limit_bytes=8 << 20),
        name="hold",
    )(x)


def product_kernel(arrived_ref, g_mine, g_other, out_ref, x_mine, x_other, sems, *, first):
    core = lax.axis_index("opt")
    columns = pl.ds(first * HALF, x_mine.shape[1])
    copies = [
        pltpu.make_async_copy(arrived_ref.at[core, :, columns], x_mine, sems.at[0]),
        pltpu.make_async_copy(arrived_ref.at[1 - core, :, columns], x_other, sems.at[1]),
    ]
    for copy in copies:
        copy.start()
    for copy in copies:
        copy.wait()

    def part(x, g):
        contract = (((0,), (0,)), ((), ()))
        p = lax.dot_general(x, g, contract, preferred_element_type=jnp.float32)
        return p.astype(jnp.bfloat16).astype(jnp.float32)

    tile = 768
    for n in range(0, out_ref.shape[1], tile):
        out_ref[:, n : n + tile] = WIRE_SCALE * (
            part(x_mine[...], g_mine[:, n : n + tile])
            + part(x_other[...], g_other[:, n : n + tile])
        )


def product(arrived, mine, other, first, count):
    slots, hidden = mine.shape
    rows = count * HALF
    vmem = pl.BlockSpec(memory_space=pltpu.VMEM)
    return pl.pallas_call(
        functools.partial(product_kernel, first=first),
        in_specs=[pl.BlockSpec(memory_space=pltpu.HBM), vmem, vmem],
        out_specs=vmem,
        scratch_shapes=[
            pltpu.VMEM((slots, rows), jnp.bfloat16),
            pltpu.VMEM((slots, rows), jnp.bfloat16),
            pltpu.SemaphoreType.DMA((2,)),
        ],
        out_shape=jax.ShapeDtypeStruct((rows, hidden), jnp.float32),
        compiler_params=pltpu.CompilerParams(vmem_limit_bytes=24 << 20),
        cost_estimate=pl.CostEstimate(
            flops=2 * 2 * slots * rows * hidden,
            bytes_accessed=4 * slots * (rows + hidden) + 4 * rows * hidden,
            transcendentals=0,
        ),
        name="product",
    )(arrived, mine, other)


def update_kernel(mask_ref, params, moment_one, moment_two, base, near, *refs, start):
    out_params, out_one, out_two = refs[-3:]
    rows, width = out_params.shape
    t = pl.program_id(0)
    for i in range(0, rows, TILE):
        for j in range(0, width, TILE):
            at = (pl.ds(i, TILE), pl.ds(pl.multiple_of(start + t * width + j, TILE), TILE))
            here = (pl.ds(i, TILE), pl.ds(pl.multiple_of(t * width + j, TILE), TILE))
            to = (pl.ds(i, TILE), pl.ds(j, TILE))
            live = mask_ref[i // TILE, (start + t * width + j) // TILE] > 0
            grad = (base[at] + near[here]) * (1.0 / WIRE_SCALE)
            weight, first, second = params[at], moment_one[at], moment_two[at]
            first_new = 0.9 * first + 0.1 * grad
            second_new = 0.95 * second + 0.05 * grad * grad
            scaled_first = first_new * (1.0 / (1.0 - 0.9**10))
            scaled_second = second_new * (1.0 / (1.0 - 0.95**10))
            step = scaled_first / (jnp.sqrt(scaled_second) + 1e-08)
            weight_new = weight - 0.01 * (step + 0.1 * weight)
            out_params[to] = jnp.where(live, weight_new, weight)
            out_one[to] = jnp.where(live, first_new, first)
            out_two[to] = jnp.where(live, second_new, second)


def update(mask, state, base, near, start, before):
    shape = base.shape
    width = 384
    done = start // width
    vmem = pl.BlockSpec(memory_space=pltpu.VMEM)
    return pl.pallas_call(
        functools.partial(update_kernel, start=start),
        grid=(near.shape[1] // width,),
        in_specs=[pl.BlockSpec(memory_space=pltpu.SMEM)]
        + [vmem] * 5
        + [pl.BlockSpec(memory_space=pl.ANY)] * len(before),
        out_specs=[pl.BlockSpec((shape[0], width), lambda t: (0, done + t))] * 3,
        out_shape=[jax.ShapeDtypeStruct(shape, jnp.float32)] * 3,
        input_output_aliases={6 + i: i for i in range(len(before))},
        compiler_params=pltpu.CompilerParams(vmem_limit_bytes=24 << 20),
        cost_estimate=pl.CostEstimate(
            flops=20 * near.size, bytes_accessed=28 * near.size, transcendentals=2 * near.size
        ),
        name="update",
    )(mask, *state, base, near, *before)


def after(x, *others):
    return lax.optimization_barrier((x,) + others)[0]


def per_device(tokens, routing, grad_gate, touched_mask, params, moment_one, moment_two):
    slots = EXPERTS * CAP
    routes = routing.T
    mine = grad_gate[0, 0, 0]
    other = lax.ppermute(mine, "opt", [(0, 1), (1, 0)])
    mine = hold(mine)

    ahead = [(i * 2 + o, ((i + (1 - 2 * o)) % N_DP) * 2 + o) for i in range(N_DP) for o in range(2)]
    across = [(i * 2 + o, ((i + (1 - 2 * o)) % N_DP) * 2 + 1 - o) for i in range(N_DP) for o in range(2)]

    def gathered(*pairs, limit=12 << 20):
        return dispatch(routes, tokens, pairs, limit)

    def exchange(sent):
        sent = sent.reshape(2 * EXPERTS, CAP, -1)
        return lax.all_to_all(sent, ("opt", "expert"), 0, 0, tiled=True).reshape(2, slots, -1)

    def totals(arrived, first, count):
        out = product(arrived, mine, other, first, count)
        return [out[j * HALF : (j + 1) * HALF] for j in range(count)]

    def plus(x, received):
        return x + received.astype(jnp.float32)

    def pack(x):
        return x.astype(jnp.float16)

    def shift(x, pairs):
        return lax.ppermute(x, ("dp", "opt"), pairs)

    sent_1 = gathered((4, 0), (3, 1), (3, 0), (2, 1), limit=60 << 20)
    arrived = exchange(sent_1)
    sent_2 = after(gathered((2, 0), (1, 1), (1, 0)), sent_1)
    sent_3 = after(gathered((0, 0)), sent_2)
    arrived, sent_2, sent_3, mine, other = lax.optimization_barrier((arrived, sent_2, sent_3, mine, other))
    four_a, three_b = totals(arrived, 0, 2)
    near_out, far_out = pack(four_a), pack(three_b)
    near = shift(near_out, ahead)
    late = exchange(after(sent_2, near_out))
    far = shift(far_out, ahead)
    three_a, two_b = totals(after(arrived, far_out), 2, 2)
    near_out = pack(plus(three_a, after(near, far_out)))
    near = shift(near_out, ahead)
    far_out = pack(plus(two_b, after(far, near_out)))
    far = shift(far_out, ahead)
    two_a, one_b, one_a = totals(late, 0, 3)
    near_out = pack(plus(two_a, after(near, far_out)))
    near = shift(near_out, ahead)
    far_out = pack(plus(one_b, after(far, near_out)))
    far = shift(far_out, across)
    last = exchange(after(sent_3, far_out))
    half = near_out.shape[1] // 2
    near = after(near, far_out)
    out_1 = pack(plus(one_a[:, :half], near[:, :half]))
    near_1 = shift(out_1, ahead)
    out_2 = pack(plus(one_a[:, half:], after(near, out_1)[:, half:]))
    near_2 = shift(out_2, ahead)
    (own,) = totals(after(last, out_1, out_2), 0, 1)
    base = plus(own, far)

    state = (params[0], moment_one[0], moment_two[0])
    outs = update(touched_mask[0], state, base, near_1.astype(jnp.float32), 0, ())
    outs = update(touched_mask[0], state, base, near_2.astype(jnp.float32), half, outs)
    return tuple(out[None] for out in outs)


def solution(mesh):
    rows = P(("dp", "expert", "opt"), None)
    state = P("expert", ("dp", "opt"), None)
    return jax.shard_map(
        per_device,
        mesh=mesh,
        in_specs=(rows, rows, P("dp", "expert", "opt", None, None), state, state, state, state),
        out_specs=(state, state, state),
        check_vma=False,
    )
```

time: 127 us -> 120 us (0.945)
  waiting for transfers between devices: 65 us -> 49.6 us
  starting transfers between devices: 19.2 us -> 25.2 us
  other arithmetic: 12.1 us -> 15.5 us
  local copies, waits for them, and re-layouts: 6.74 us -> 3.57 us
  Pallas kernels: 22.5 us -> 24.9 us
    ppermute x7 -> x8, waiting for transfers between devices: 39.1 us -> 15.1 us  [shift(): return lax.ppermute(x, ('dp', 'opt'), pairs)]
    all_to_all x2 -> x3, waiting for transfers between devices: 25.9 us -> 34.4 us  [exchange(): lax.all_to_all(sent, ('opt', 'expert'), 0, 0, tiled=True)]
    all_to_all x2 -> x3, starting transfers between devices: 15.5 us -> 22.3 us  [exchange(): lax.all_to_all(sent, ('opt', 'expert'), 0, 0, tiled=True)]
    broadcast_in_dim x1 -> x0, other arithmetic: 6.52 us -> none  [per_device(): out_second = jnp.where(live, second_new, second)[None]]
    convert_element_type x6, other arithmetic: 5.45 us -> 11.7 us  [pack(): return x.astype(jnp.float16)]
    pallas_call x6 -> x10, Pallas kernels: 22.5 us -> 24.9 us  [the longest x4 12.3 us: product(): pl.pallas_call(functools.partial(product_kernel, first=first), in_specs=[...]
    convert_element_type x0 -> x2, other arithmetic: none -> 2.1 us  [the longest x1 1.05 us: per_device(): near_1.astype(jnp.float32)]
    gt x2 -> x0, local copies, waits for them, and re-layouts: 1.66 us -> none  [per_device(): jnp.repeat(jnp.repeat(touched_mask[0], TILE, axis=0), TILE, axis=1) > 0]
  transfers between devices with their start and end apart: 10 -> 12, of which waited for: 8 -> 9; matrix products, arithmetic and copies ran while one was open for 7% -> 12% of each run, Pallas kernels for 13% -> 13%
where the time goes in v2:
time: 120 us
  waiting for transfers between devices  49.6 us (41%)
  starting transfers between devices  25.2 us (21%)
  Pallas kernels  24.9 us (21%)
  other arithmetic  15.5 us (13%)
  local copies, waits for them, and re-layouts  3.57 us (3%)
    all_to_all x3, waiting for transfers between devices, exchange(): lax.all_to_all(sent, ('opt', 'expert'), 0, 0, tiled=True)  34.4 us
    all_to_all x3, starting transfers between devices, exchange(): lax.all_to_all(sent, ('opt', 'expert'), 0, 0, tiled=True)  22.3 us
    ppermute x8, waiting for transfers between devices, shift(): return lax.ppermute(x, ('dp', 'opt'), pairs)  15.1 us
    pallas_call x4, Pallas kernels, product(): pl.pallas_call(functools.partial(product_kernel, first=first), in_specs=[...  12.3 us
    convert_element_type x6, other arithmetic, pack(): return x.astype(jnp.float16)  11.7 us
    pallas_call x3, Pallas kernels, dispatch(): pl.pallas_call(functools.partial(dispatch_kernel, pairs=pairs), in_specs=...  6.01 us
    pallas_call x2, Pallas kernels, update(): pl.pallas_call(functools.partial(update_kernel, start=start), grid=(near....  4.96 us
    ppermute x8, starting transfers between devices, shift(): return lax.ppermute(x, ('dp', 'opt'), pairs)  2.63 us
  transfers between devices with their start and end apart: 12, of which 9 were waited for; matrix products, arithmetic and copies ran while one was open for 12% of the time, Pallas kernels for 13%

profile of v2, /device:TPU:2, one launch (start us, length us, event | category | flops | bytes accessed | tf_op | source)
XLA Modules:
  0.0 119.6 jit_solution(7851674367723540104)
XLA Ops:
  0.6 3.8 %dispatch.3 = bf16[1024,1024]{1,0:T(8,128)(2,1)} custom-call(s32[8,256]{1,0:T(8,128)} %bitcast.23, bf16[256,4096]{1,0:T(8,128)(2,1)} %tokens_ref.5), custom_call_target="tpu_custom_call" | custom-call | flops 536870912 | bytes 3145728 | tf_op jit(solution)/shard_map/dispatch/pallas_call | solution.py:80
  4.4 7.7 %all-to-all-start = ((bf16[32,32,1024]{2,1,0:T(8,128)(2,1)}), bf16[32,32,1024]{2,1,0:T(8,128)(2,1)}, u32[]{:S(2)}, u32[]{:S(2)}) async-start(bf16[32,32,1024]{2,1,0:T(8,128)(2,1)} %bitcast.28), calls=%async_computation | async-start | bytes 4194304 | tf_op jit(solution)/shard_map/all_to_all | solution.py:231
  12.4 1.6 %hold.1.g_mine = bf16[512,1536]{1,0:T(8,128)(2,1)S(1)} custom-call(bf16[512,1536]{1,0:T(8,128)(2,1)} %bitcast.7.x_ref), custom_call_target="tpu_custom_call" | custom-call | tf_op jit(solution)/shard_map/hold/pallas_call | solution.py:108
  14.2 1.4 %dispatch.4 = bf16[1024,768]{1,0:T(8,128)(2,1)S(1)} custom-call(s32[8,256]{1,0:T(8,128)S(1)} %bitcast.24, bf16[256,4096]{1,0:T(8,128)(2,1)S(1)} %copy-done.1), custom_call_target="tpu_custom_call" | custom-call | flops 402653184 | bytes 2359296 | tf_op jit(solution)/shard_map/dispatch/pallas_call | solution.py:80
  15.5 1.1 copy-done.2
  16.7 0.9 dispatch.5
  18.4 23.0 %all-to-all-done = bf16[32,32,1024]{2,1,0:T(8,128)(2,1)} async-done(((bf16[32,32,1024]{2,1,0:T(8,128)(2,1)}), bf16[32,32,1024]{2,1,0:T(8,128)(2,1)}, u32[]{:S(2)}, u32[]{:S(2)}) %all-to-all-start) | async-done | bytes 2097184 | tf_op jit(solution)/shard_map/all_to_all | solution.py:231
  41.4 3.1 %product.4 = f32[512,1536]{1,0:T(8,128)S(1)} custom-call(bf16[2,512,1024]{2,1,0:T(8,128)(2,1)} %bitcast.6.arrived_ref, bf16[512,1536]{1,0:T(8,128)(2,1)S(1)} %hold.1.g_mine, bf16[512,1536]{1,0:T(8,128)(2,1)S(1)} %collective-permute-done.g_other), custom_call_target="tpu_custom_call" | custom-call | flops 1610612736 | bytes 7340032 | tf_op jit(solution)/shard_map/product/pallas_call | solution.py:147
  44.7 1.4 %fusion.6 = (f16[256,1536]{1,0:T(8,128)(2,1)}, f16[256,1536]{1,0:T(8,128)(2,1)}) fusion(f16[512,1536]{1,0:T(8,128)(2,1)S(1)} %convert.4), kind=kLoop, calls=%fused_computation.13 | loop fusion | bytes 3145728 | tf_op jit(solution)/shard_map/slice | solution.py:235
  46.1 1.9 %collective-permute-start.2 = (f16[256,1536]{1,0:T(8,128)(2,1)}, f16[256,1536]{1,0:T(8,128)(2,1)}, u32[]{:S(2)}, u32[]{:S(2)}) collective-permute-start(f16[256,1536]{1,0:T(8,128)(2,1)} %get-tuple-element.50), channel_id=1, source_target_pairs={{0,32},{1,225},{32,64},{33,1},{64,96},{65,33},{96,128},{97,65},{12... | collective-permute-start | bytes 2359304 | tf_op jit(solution)/shard_map/ppermute | solution.py:244
  48.0 7.9 %all-to-all-start.1 = ((bf16[32,32,768]{2,1,0:T(8,128)(2,1)}), bf16[32,32,768]{2,1,0:T(8,128)(2,1)}, u32[]{:S(2)}, u32[]{:S(2)}) async-start(bf16[32,32,768]{2,1,0:T(8,128)(2,1)} %bitcast.15), calls=%async_computation.1 | async-start | bytes 3145728 | tf_op jit(solution)/shard_map/all_to_all | solution.py:231
  56.0 3.1 %product.6 = f32[512,1536]{1,0:T(8,128)S(1)} custom-call(bf16[2,512,1024]{2,1,0:T(8,128)(2,1)} %bitcast.6.arrived_ref, bf16[512,1536]{1,0:T(8,128)(2,1)S(1)} %hold.1.g_mine, bf16[512,1536]{1,0:T(8,128)(2,1)S(1)} %collective-permute-done.g_other), custom_call_target="tpu_custom_call" | custom-call | flops 1610612736 | bytes 7340032 | tf_op jit(solution)/shard_map/product/pallas_call | solution.py:147
  59.1 3.1 %collective-permute-done.2 = f16[256,1536]{1,0:T(8,128)(2,1)} collective-permute-done((f16[256,1536]{1,0:T(8,128)(2,1)}, f16[256,1536]{1,0:T(8,128)(2,1)}, u32[]{:S(2)}, u32[]{:S(2)}) %collective-permute-start.2) | collective-permute-done | bytes 786464 | tf_op jit(solution)/shard_map/ppermute | solution.py:244
  62.3 2.2 %fusion.1 = f16[256,1536]{1,0:T(8,128)(2,1)} fusion(f32[512,1536]{1,0:T(8,128)S(1)} %product.6, f16[256,1536]{1,0:T(8,128)(2,1)} %collective-permute-done.2), kind=kLoop, calls=%fused_computation.3 | loop fusion | flops 1179648 | bytes 3145728 | tf_op jit(solution)/shard_map/convert_element_type | solution.py:241
  64.5 6.1 %collective-permute-done.1 = f16[256,1536]{1,0:T(8,128)(2,1)S(1)} collective-permute-done((f16[256,1536]{1,0:T(8,128)(2,1)}, f16[256,1536]{1,0:T(8,128)(2,1)S(1)}, u32[]{:S(2)}, u32[]{:S(2)}) %collective-permute-start.1) | collective-permute-done | bytes 786464 | tf_op jit(solution)/shard_map/ppermute | solution.py:244
  70.6 1.1 fusion.2
  71.7 7.1 %all-to-all-done.1 = bf16[32,32,768]{2,1,0:T(8,128)(2,1)} async-done(((bf16[32,32,768]{2,1,0:T(8,128)(2,1)}), bf16[32,32,768]{2,1,0:T(8,128)(2,1)}, u32[]{:S(2)}, u32[]{:S(2)}) %all-to-all-start.1) | async-done | bytes 1572896 | tf_op jit(solution)/shard_map/all_to_all | solution.py:231
  78.8 4.1 %product.5 = f32[768,1536]{1,0:T(8,128)S(1)} custom-call(bf16[2,512,768]{2,1,0:T(8,128)(2,1)} %bitcast.9.arrived_ref, bf16[512,1536]{1,0:T(8,128)(2,1)S(1)} %hold.1.g_mine, bf16[512,1536]{1,0:T(8,128)(2,1)S(1)} %collective-permute-done.g_other), custom_call_target="tpu_custom_call" | custom-call | flops 2415919104 | bytes 9437184 | tf_op jit(solution)/shard_map/product/pallas_call | solution.py:147
  82.9 2.8 %fusion = f16[256,1536]{1,0:T(8,128)(2,1)} fusion(f32[768,1536]{1,0:T(8,128)S(1)} %product.5, f16[256,1536]{1,0:T(8,128)(2,1)} %collective-permute-done.4), kind=kLoop, calls=%fused_computation.1 | loop fusion | flops 1179648 | bytes 3145728 | tf_op jit(solution)/shard_map/convert_element_type | solution.py:241
  85.7 1.8 %collective-permute-done.3 = f16[256,1536]{1,0:T(8,128)(2,1)} collective-permute-done((f16[256,1536]{1,0:T(8,128)(2,1)}, f16[256,1536]{1,0:T(8,128)(2,1)}, u32[]{:S(2)}, u32[]{:S(2)}) %collective-permute-start.3) | collective-permute-done | bytes 786464 | tf_op jit(solution)/shard_map/ppermute | solution.py:244
  87.5 2.2 %fusion.3 = f16[256,1536]{1,0:T(8,128)(2,1)} fusion(f32[768,1536]{1,0:T(8,128)S(1)} %product.5, f16[256,1536]{1,0:T(8,128)(2,1)} %collective-permute-done.3), kind=kLoop, calls=%fused_computation.7 | loop fusion | flops 1179648 | bytes 3145728 | tf_op jit(solution)/shard_map/convert_element_type | solution.py:241
  89.8 6.7 %all-to-all-start.2 = ((bf16[32,32,256]{2,1,0:T(8,128)(2,1)}), bf16[32,32,256]{2,1,0:T(8,128)(2,1)}, u32[]{:S(2)}, u32[]{:S(2)}) async-start(bf16[32,32,256]{2,1,0:T(8,128)(2,1)} %bitcast.22), calls=%async_computation.2 | async-start | bytes 1048576 | tf_op jit(solution)/shard_map/all_to_all | solution.py:231
  96.5 2.7 %collective-permute-done.5 = f16[256,1536]{1,0:T(8,128)(2,1)} collective-permute-done((f16[256,1536]{1,0:T(8,128)(2,1)}, f16[256,1536]{1,0:T(8,128)(2,1)}, u32[]{:S(2)}, u32[]{:S(2)}) %collective-permute-start.5) | collective-permute-done | bytes 786464 | tf_op jit(solution)/shard_map/ppermute | solution.py:244
  99.2 2.1 %fusion.5 = f16[256,768]{1,0:T(8,128)(2,1)} fusion(f32[768,1536]{1,0:T(8,128)} %copy-done, f16[256,1536]{1,0:T(8,128)(2,1)} %collective-permute-done.5), kind=kLoop, calls=%fused_computation.12 | loop fusion | flops 589824 | bytes 1572864 | tf_op jit(solution)/shard_map/convert_element_type | solution.py:241
  101.3 1.3 %fusion.4 = f16[256,768]{1,0:T(8,128)(2,1)S(1)} fusion(f32[768,1536]{1,0:T(8,128)} %copy-done, f16[256,1536]{1,0:T(8,128)(2,1)} %collective-permute-done.5), kind=kLoop, calls=%fused_computation.10 | loop fusion | flops 589824 | bytes 1572864 | tf_op jit(solution)/shard_map/convert_element_type | solution.py:241
  103.2 4.3 %all-to-all-done.2 = bf16[32,32,256]{2,1,0:T(8,128)(2,1)} async-done(((bf16[32,32,256]{2,1,0:T(8,128)(2,1)}), bf16[32,32,256]{2,1,0:T(8,128)(2,1)}, u32[]{:S(2)}, u32[]{:S(2)}) %all-to-all-start.2) | async-done | bytes 524320 | tf_op jit(solution)/shard_map/all_to_all | solution.py:231
  107.5 2.1 %product.7 = f32[256,1536]{1,0:T(8,128)S(1)} custom-call(bf16[2,512,256]{2,1,0:T(8,128)(2,1)} %bitcast.11.arrived_ref, bf16[512,1536]{1,0:T(8,128)(2,1)S(1)} %hold.1.g_mine, bf16[512,1536]{1,0:T(8,128)(2,1)S(1)} %collective-permute-done.g_other), custom_call_target="tpu_custom_call" | custom-call | flops 805306368 | bytes 5242880 | tf_op jit(solution)/shard_map/product/pallas_call | solution.py:147
  109.7 1.5 %convert_add_fusion.base = f32[256,1536]{1,0:T(8,128)S(1)} fusion(f32[256,1536]{1,0:T(8,128)S(1)} %product.7, f16[256,1536]{1,0:T(8,128)(2,1)} %collective-permute-done.6), kind=kLoop, calls=%fused_computation.8 | loop fusion | flops 786432 | bytes 3932160 | tf_op jit(solution)/shard_map/add | solution.py:238
  111.9 1.0 convert_element_type.61.near
  113.0 2.5 %update.2 = (f32[256,1536]{1,0:T(8,128)}, f32[256,1536]{1,0:T(8,128)}, f32[256,1536]{1,0:T(8,128)}) custom-call(s32[2,12]{1,0:T(2,128)S(1)} %bitcast.26, f32[256,1536]{1,0:T(8,128)S(1)} %bitcast.16, f32[256,1536]{1,0:T(8,128)S(1)} %bitcast.18, f32[256,1536]{1,0:T(8,128)S(1)} %bitcast.20, f32[256,1536]{1,0:T(8,128)S(1)} %convert_add_fusion.base, ...), custom_call_target="tpu_custom_call" | custom-call | flops 3932160 | bytes 5505024 | tf_op jit(solution)/shard_map/update/pallas_call | solution.py:195
  116.1 1.0 convert_element_type.60.near
  117.1 2.5 %update.3 = (f32[256,1536]{1,0:T(8,128)}, f32[256,1536]{1,0:T(8,128)}, f32[256,1536]{1,0:T(8,128)}) custom-call(s32[2,12]{1,0:T(2,128)S(1)} %bitcast.27, f32[256,1536]{1,0:T(8,128)S(1)} %bitcast.17, f32[256,1536]{1,0:T(8,128)S(1)} %bitcast.19, f32[256,1536]{1,0:T(8,128)S(1)} %bitcast.21, ...), custom_call_target="tpu_custom_call", output_to_operand_aliasing={{0}: (6, {}), {1}: (7, {}), {2}: (8, {})} | custom-call | flops 3932160 | bytes 5505024 | tf_op jit(solution)/shard_map/update/pallas_call | solution.py:195
  (31 shorter events, 3.6 us)
Async XLA Ops:
  4.4 37.0 %all-to-all-start = ((bf16[32,32,1024]{2,1,0:T(8,128)(2,1)}), bf16[32,32,1024]{2,1,0:T(8,128)(2,1)}, u32[]{:S(2)}, u32[]{:S(2)}) async-start(bf16[32,32,1024]{2,1,0:T(8,128)(2,1)} %bitcast.28), calls=%async_computation | async-start | bytes 4194304 | tf_op jit(solution)/shard_map/all_to_all | solution.py:231
  12.1 2.1 %copy-start.1 = (bf16[256,4096]{1,0:T(8,128)(2,1)S(1)}, bf16[256,4096]{1,0:T(8,128)(2,1)}, u32[]{:S(2)}) copy-start(bf16[256,4096]{1,0:T(8,128)(2,1)} %tokens_ref.5) | copy-start | bytes 6291460
  12.1 2.1 %copy-start.7 = (s32[256,8]{0,1:T(8,128)S(1)}, s32[256,8]{0,1:T(8,128)}, u32[]{:S(2)}) copy-start(s32[256,8]{0,1:T(8,128)} %param.8) | copy-start | bytes 24580
  12.1 6.3 %collective-permute-start = (bf16[512,1536]{1,0:T(8,128)(2,1)}, bf16[512,1536]{1,0:T(8,128)(2,1)S(1)}, u32[]{:S(2)}, u32[]{:S(2)}) collective-permute-start(bf16[512,1536]{1,0:T(8,128)(2,1)} %bitcast.7.x_ref), channel_id=1, source_target_pairs={{0,1},{1,0},{2,3},{3,2},{4,5},{5,4},{6,7},{7,6},{8,9},{9,8},{10,11... | collective-permute-start | bytes 4718600 | tf_op jit(solution)/shard_map/ppermute | solution.py:220
  15.5 1.1 copy-start.2
  17.6 0.8 copy-start.6
  46.1 16.1 %collective-permute-start.2 = (f16[256,1536]{1,0:T(8,128)(2,1)}, f16[256,1536]{1,0:T(8,128)(2,1)}, u32[]{:S(2)}, u32[]{:S(2)}) collective-permute-start(f16[256,1536]{1,0:T(8,128)(2,1)} %get-tuple-element.50), channel_id=1, source_target_pairs={{0,32},{1,225},{32,64},{33,1},{64,96},{65,33},{96,128},{97,65},{12... | collective-permute-start | bytes 2359304 | tf_op jit(solution)/shard_map/ppermute | solution.py:244
  48.0 30.8 %all-to-all-start.1 = ((bf16[32,32,768]{2,1,0:T(8,128)(2,1)}), bf16[32,32,768]{2,1,0:T(8,128)(2,1)}, u32[]{:S(2)}, u32[]{:S(2)}) async-start(bf16[32,32,768]{2,1,0:T(8,128)(2,1)} %bitcast.15), calls=%async_computation.1 | async-start | bytes 3145728 | tf_op jit(solution)/shard_map/all_to_all | solution.py:231
  56.0 14.6 %collective-permute-start.1 = (f16[256,1536]{1,0:T(8,128)(2,1)}, f16[256,1536]{1,0:T(8,128)(2,1)S(1)}, u32[]{:S(2)}, u32[]{:S(2)}) collective-permute-start(f16[256,1536]{1,0:T(8,128)(2,1)} %get-tuple-element.49), channel_id=1, source_target_pairs={{0,32},{1,225},{32,64},{33,1},{64,96},{65,33},{96,128},{97,65},{12... | collective-permute-start | bytes 2359304 | tf_op jit(solution)/shard_map/ppermute | solution.py:244
  64.5 18.4 %collective-permute-start.4 = (f16[256,1536]{1,0:T(8,128)(2,1)}, f16[256,1536]{1,0:T(8,128)(2,1)}, u32[]{:S(2)}, u32[]{:S(2)}) collective-permute-start(f16[256,1536]{1,0:T(8,128)(2,1)} %fusion.1), channel_id=1, source_target_pairs={{0,32},{1,225},{32,64},{33,1},{64,96},{65,33},{96,128},{97,65},{12... | collective-permute-start | bytes 2359304 | tf_op jit(solution)/shard_map/ppermute | solution.py:244
  71.7 15.9 %collective-permute-start.3 = (f16[256,1536]{1,0:T(8,128)(2,1)}, f16[256,1536]{1,0:T(8,128)(2,1)}, u32[]{:S(2)}, u32[]{:S(2)}) collective-permute-start(f16[256,1536]{1,0:T(8,128)(2,1)} %fusion.2), channel_id=1, source_target_pairs={{0,32},{1,225},{32,64},{33,1},{64,96},{65,33},{96,128},{97,65},{12... | collective-permute-start | bytes 2359304 | tf_op jit(solution)/shard_map/ppermute | solution.py:244
  82.9 4.7 %copy-start = (f32[768,1536]{1,0:T(8,128)}, f32[768,1536]{1,0:T(8,128)S(1)}, u32[]{:S(2)}) copy-start(f32[768,1536]{1,0:T(8,128)S(1)} %product.5) | copy-start | bytes 14155780
  85.7 13.5 %collective-permute-start.5 = (f16[256,1536]{1,0:T(8,128)(2,1)}, f16[256,1536]{1,0:T(8,128)(2,1)}, u32[]{:S(2)}, u32[]{:S(2)}) collective-permute-start(f16[256,1536]{1,0:T(8,128)(2,1)} %fusion), channel_id=1, source_target_pairs={{0,32},{1,225},{32,64},{33,1},{64,96},{65,33},{96,128},{97,65},{12... | collective-permute-start | bytes 2359304 | tf_op jit(solution)/shard_map/ppermute | solution.py:244
  89.8 19.8 %collective-permute-start.6 = (f16[256,1536]{1,0:T(8,128)(2,1)}, f16[256,1536]{1,0:T(8,128)(2,1)}, u32[]{:S(2)}, u32[]{:S(2)}) collective-permute-start(f16[256,1536]{1,0:T(8,128)(2,1)} %fusion.3), channel_id=1, source_target_pairs={{0,33},{1,224},{32,65},{33,0},{64,97},{65,32},{96,129},{97,64},{12... | collective-permute-start | bytes 2359304 | tf_op jit(solution)/shard_map/ppermute | solution.py:244
  89.8 17.7 %all-to-all-start.2 = ((bf16[32,32,256]{2,1,0:T(8,128)(2,1)}), bf16[32,32,256]{2,1,0:T(8,128)(2,1)}, u32[]{:S(2)}, u32[]{:S(2)}) async-start(bf16[32,32,256]{2,1,0:T(8,128)(2,1)} %bitcast.22), calls=%async_computation.2 | async-start | bytes 1048576 | tf_op jit(solution)/shard_map/all_to_all | solution.py:231
  101.3 10.6 %collective-permute-start.8 = (f16[256,768]{1,0:T(8,128)(2,1)}, f16[256,768]{1,0:T(8,128)(2,1)}, u32[]{:S(2)}, u32[]{:S(2)}) collective-permute-start(f16[256,768]{1,0:T(8,128)(2,1)} %fusion.5), channel_id=1, source_target_pairs={{0,32},{1,225},{32,64},{33,1},{64,96},{65,33},{96,128},{97,65},{12... | collective-permute-start | bytes 1179656 | tf_op jit(solution)/shard_map/ppermute | solution.py:244
  102.6 13.4 %collective-permute-start.7 = (f16[256,768]{1,0:T(8,128)(2,1)S(1)}, f16[256,768]{1,0:T(8,128)(2,1)}, u32[]{:S(2)}, u32[]{:S(2)}) collective-permute-start(f16[256,768]{1,0:T(8,128)(2,1)S(1)} %fusion.4), channel_id=1, source_target_pairs={{0,32},{1,225},{32,64},{33,1},{64,96},{65,33},{96,128},{97,65},{12... | collective-permute-start | bytes 1179656 | tf_op jit(solution)/shard_map/ppermute | solution.py:244
  109.6 3.3 %copy-start.8 = (s32[1,2,12]{2,1,0:T(2,128)S(1)}, s32[1,2,12]{2,1,0:T(2,128)}, u32[]{:S(2)}) copy-start(s32[1,2,12]{2,1,0:T(2,128)} %param.10) | copy-start | bytes 292
  109.6 3.3 %copy-start.3 = (f32[1,256,1536]{2,1,0:T(8,128)S(1)}, f32[1,256,1536]{2,1,0:T(8,128)}, u32[]{:S(2)}) copy-start(f32[1,256,1536]{2,1,0:T(8,128)} %param.11) | copy-start | bytes 4718596
  109.6 3.3 %copy-start.4 = (f32[1,256,1536]{2,1,0:T(8,128)S(1)}, f32[1,256,1536]{2,1,0:T(8,128)}, u32[]{:S(2)}) copy-start(f32[1,256,1536]{2,1,0:T(8,128)} %param.12) | copy-start | bytes 4718596
  109.6 3.3 %copy-start.5 = (f32[1,256,1536]{2,1,0:T(8,128)S(1)}, f32[1,256,1536]{2,1,0:T(8,128)}, u32[]{:S(2)}) copy-start(f32[1,256,1536]{2,1,0:T(8,128)} %param.13) | copy-start | bytes 4718596

commit v3 on v2

--- a/solution.py
+++ b/solution.py
@@ -32,33 +32,34 @@
     ).astype(jnp.bfloat16)
 
 
-def columns_of(r, core, pairs):
+def columns_of(r, core, blocks):
     starts = []
-    for distance, other in pairs:
+    for distance, other, offset, _ in blocks:
         up = 2 * lax.rem(r + distance, N_DP) + other
         down = 2 * lax.rem(r + (N_DP - distance), N_DP) + 1 - other
-        block = jnp.where(core == 0, up, down)
-        starts.append(pl.multiple_of(block * HALF, HALF))
+        starts.append(pl.multiple_of(jnp.where(core == 0, up, down) * HALF + offset, 128))
     return starts
 
 
-def dispatch_kernel(routes_ref, tokens_ref, out_ref, tokens_in, pick_ref, made, in_sems, out_sems, *, pairs):
-    starts = columns_of(lax.axis_index("dp"), 0, pairs) + columns_of(lax.axis_index("dp"), 1, pairs)
-    reads = [
-        pltpu.make_async_copy(
-            tokens_ref.at[:, pl.ds(start, HALF)],
-            tokens_in.at[n // len(pairs), :, pl.ds(n % len(pairs) * HALF, HALF)],
-            in_sems.at[n],
-        )
-        for n, start in enumerate(starts)
-    ]
-    for read in reads:
-        read.start()
+def dispatch_kernel(routes_ref, tokens_ref, out_ref, tokens_in, pick_ref, made, in_sems, out_sems, *, blocks):
+    r = lax.axis_index("dp")
+    reads = []
+    for core in range(2):
+        place = 0
+        for (*_, width), start in zip(blocks, columns_of(r, core, blocks)):
+            read = pltpu.make_async_copy(
+                tokens_ref.at[:, pl.ds(start, width)],
+                tokens_in.at[core, :, pl.ds(place, width)],
+                in_sems.at[len(reads)],
+            )
+            read.start()
+            reads.append(read)
+            place = place + width
     pick_ref[...] = picks(routes_ref[...], tokens_ref.shape[0])
     rows = EXPERTS * CAP
     writes = []
     for core in range(2):
-        for read in reads[core * len(pairs) : (core + 1) * len(pairs)]:
+        for read in reads[core * len(blocks) : (core + 1) * len(blocks)]:
             read.wait()
         made[core] = jnp.dot(
             pick_ref[...], tokens_in[core], preferred_element_type=jnp.float32
@@ -72,28 +73,26 @@
         write.wait()
 
 
-def dispatch(routes, tokens, pairs, limit):
+def dispatch(routes, tokens, blocks, limit):
     rows = EXPERTS * CAP
     count = tokens.shape[0]
-    blocks = 2 * len(pairs)
+    total = sum(width for *_, width in blocks)
     hbm = pl.BlockSpec(memory_space=pltpu.HBM)
     return pl.pallas_call(
-        functools.partial(dispatch_kernel, pairs=pairs),
+        functools.partial(dispatch_kernel, blocks=blocks),
         in_specs=[pl.BlockSpec(memory_space=pltpu.VMEM), hbm],
         out_specs=hbm,
         scratch_shapes=[
-            pltpu.VMEM((2, count, len(pairs) * HALF), jnp.bfloat16),
+            pltpu.VMEM((2, count, total), jnp.bfloat16),
             pltpu.VMEM((rows, count), jnp.bfloat16),
-            pltpu.VMEM((2, rows, len(pairs) * HALF), jnp.bfloat16),
-            pltpu.SemaphoreType.DMA((blocks,)),
+            pltpu.VMEM((2, rows, total), jnp.bfloat16),
+            pltpu.SemaphoreType.DMA((2 * len(blocks),)),
             pltpu.SemaphoreType.DMA((2,)),
         ],
-        out_shape=jax.ShapeDtypeStruct((2 * rows, len(pairs) * HALF), jnp.bfloat16),
+        out_shape=jax.ShapeDtypeStruct((2 * rows, total), jnp.bfloat16),
         compiler_params=pltpu.CompilerParams(vmem_limit_bytes=limit),
         cost_estimate=pl.CostEstimate(
-            flops=2 * rows * blocks * HALF * count,
-            bytes_accessed=blocks * HALF * (count + rows) * 2,
-            transcendentals=0,
+            flops=4 * rows * total * count, bytes_accessed=4 * total * (count + rows), transcendentals=0
         ),
         name="dispatch",
     )(routes, tokens)
@@ -117,7 +116,7 @@
 
 def product_kernel(arrived_ref, g_mine, g_other, out_ref, x_mine, x_other, sems, *, first):
     core = lax.axis_index("opt")
-    columns = pl.ds(first * HALF, x_mine.shape[1])
+    columns = pl.ds(first, x_mine.shape[1])
     copies = [
         pltpu.make_async_copy(arrived_ref.at[core, :, columns], x_mine, sems.at[0]),
         pltpu.make_async_copy(arrived_ref.at[1 - core, :, columns], x_other, sems.at[1]),
@@ -140,9 +139,8 @@
         )
 
 
-def product(arrived, mine, other, first, count):
+def product(arrived, mine, other, first, rows):
     slots, hidden = mine.shape
-    rows = count * HALF
     vmem = pl.BlockSpec(memory_space=pltpu.VMEM)
     return pl.pallas_call(
         functools.partial(product_kernel, first=first),
@@ -223,16 +221,16 @@
     ahead = [(i * 2 + o, ((i + (1 - 2 * o)) % N_DP) * 2 + o) for i in range(N_DP) for o in range(2)]
     across = [(i * 2 + o, ((i + (1 - 2 * o)) % N_DP) * 2 + 1 - o) for i in range(N_DP) for o in range(2)]
 
-    def gathered(*pairs, limit=12 << 20):
-        return dispatch(routes, tokens, pairs, limit)
+    def gathered(*blocks, limit=12 << 20):
+        return dispatch(routes, tokens, blocks, limit)
 
     def exchange(sent):
         sent = sent.reshape(2 * EXPERTS, CAP, -1)
         return lax.all_to_all(sent, ("opt", "expert"), 0, 0, tiled=True).reshape(2, slots, -1)
 
-    def totals(arrived, first, count):
-        out = product(arrived, mine, other, first, count)
-        return [out[j * HALF : (j + 1) * HALF] for j in range(count)]
+    def totals(arrived, first, *widths):
+        out = product(arrived, mine, other, first, sum(widths))
+        return jnp.split(out, [sum(widths[:j]) for j in range(1, len(widths))]) if len(widths) > 1 else [out]
 
     def plus(x, received):
         return x + received.astype(jnp.float32)
@@ -243,34 +241,40 @@
     def shift(x, pairs):
         return lax.ppermute(x, ("dp", "opt"), pairs)
 
-    sent_1 = gathered((4, 0), (3, 1), (3, 0), (2, 1), limit=60 << 20)
+    some = HALF // 2
+    sent_1 = gathered((4, 0, 0, HALF), (3, 1, 0, HALF), (3, 0, 0, some), limit=60 << 20)
     arrived = exchange(sent_1)
-    sent_2 = after(gathered((2, 0), (1, 1), (1, 0)), sent_1)
-    sent_3 = after(gathered((0, 0)), sent_2)
+    sent_2 = after(gathered((3, 0, some, some), (2, 1, 0, HALF), (2, 0, 0, HALF), (1, 1, 0, HALF)), sent_1)
+    sent_3 = after(gathered((1, 0, 0, HALF), (0, 0, 0, HALF)), sent_2)
     arrived, sent_2, sent_3, mine, other = lax.optimization_barrier((arrived, sent_2, sent_3, mine, other))
-    four_a, three_b = totals(arrived, 0, 2)
+    late = exchange(sent_2)
+    four_a, three_b = totals(arrived, 0, HALF, HALF)
     near_out, far_out = pack(four_a), pack(three_b)
     near = shift(near_out, ahead)
-    late = exchange(after(sent_2, near_out))
     far = shift(far_out, ahead)
-    three_a, two_b = totals(after(arrived, far_out), 2, 2)
-    near_out = pack(plus(three_a, after(near, far_out)))
-    near = shift(near_out, ahead)
+    (three_a,) = totals(after(arrived, far_out), 2 * HALF, some)
+    near = after(near, three_a)
+    near_out = pack(plus(three_a, near[:some]))
+    near_1 = shift(near_out, ahead)
+    three_a, two_b = totals(after(late, near_out), 0, some, HALF)
+    near_out = pack(plus(three_a, near[some:]))
+    near_2 = shift(near_out, ahead)
     far_out = pack(plus(two_b, after(far, near_out)))
     far = shift(far_out, ahead)
-    two_a, one_b, one_a = totals(late, 0, 3)
-    near_out = pack(plus(two_a, after(near, far_out)))
+    last = exchange(after(sent_3, far_out))
+    two_a, one_b = totals(after(late, far_out), some + HALF, HALF, HALF)
+    near = after(jnp.concatenate([near_1, near_2]), two_a)
+    near_out = pack(plus(two_a, near))
     near = shift(near_out, ahead)
     far_out = pack(plus(one_b, after(far, near_out)))
     far = shift(far_out, across)
-    last = exchange(after(sent_3, far_out))
+    one_a, own = totals(after(last, far_out), 0, HALF, HALF)
     half = near_out.shape[1] // 2
     near = after(near, far_out)
     out_1 = pack(plus(one_a[:, :half], near[:, :half]))
     near_1 = shift(out_1, ahead)
     out_2 = pack(plus(one_a[:, half:], after(near, out_1)[:, half:]))
     near_2 = shift(out_2, ahead)
-    (own,) = totals(after(last, out_1, out_2), 0, 1)
     base = plus(own, far)
 
     state = (params[0], moment_one[0], moment_two[0])

time: 120 us -> 118 us (0.983)
  waiting for transfers between devices: 49.6 us -> 40.8 us
  starting transfers between devices: 25.2 us -> 32.3 us
  other arithmetic: 15.5 us -> 12.5 us
  local copies, waits for them, and re-layouts: 3.57 us -> 6.32 us
    all_to_all x3, waiting for transfers between devices: 34.4 us -> 23.6 us  [exchange(): lax.all_to_all(sent, ('opt', 'expert'), 0, 0, tiled=True)]
    ppermute x8 -> x9, starting transfers between devices: 2.63 us -> 12.4 us  [shift(): return lax.ppermute(x, ('dp', 'opt'), pairs)]
    unnamed x18 -> x22, local copies, waits for them, and re-layouts: 2.14 us -> 5.15 us
    all_to_all x3, starting transfers between devices: 22.3 us -> 19.8 us  [exchange(): lax.all_to_all(sent, ('opt', 'expert'), 0, 0, tiled=True)]
    convert_element_type x6 -> x7, other arithmetic: 11.7 us -> 9.56 us  [pack(): return x.astype(jnp.float16)]
    ppermute x8 -> x9, waiting for transfers between devices: 15.1 us -> 17.3 us  [shift(): return lax.ppermute(x, ('dp', 'opt'), pairs)]
    pallas_call x1, Pallas kernels: 1.63 us -> 0.1 us  [hold(): pl.pallas_call(hold_kernel, in_specs=[vmem], out_specs=vmem, out_shape=ja...]
    slice x1 -> x0, local copies, waits for them, and re-layouts: 1.43 us -> none  [totals(): return [out[j * HALF:(j + 1) * HALF] for j in range(count)]]
  transfers between devices with their start and end apart: 12 -> 13, of which waited for: 9 -> 7; matrix products, arithmetic and copies ran while one was open for 12% -> 12% of each run, Pallas kernels for 13% -> 19%
where the time goes in v3:
time: 118 us
  waiting for transfers between devices  40.8 us (35%)
  starting transfers between devices  32.3 us (27%)
  Pallas kernels  24.9 us (21%)
  other arithmetic  12.5 us (11%)
  local copies, waits for them, and re-layouts  6.32 us (5%)
    all_to_all x3, waiting for transfers between devices, exchange(): lax.all_to_all(sent, ('opt', 'expert'), 0, 0, tiled=True)  23.6 us
    all_to_all x3, starting transfers between devices, exchange(): lax.all_to_all(sent, ('opt', 'expert'), 0, 0, tiled=True)  19.8 us
    ppermute x9, waiting for transfers between devices, shift(): return lax.ppermute(x, ('dp', 'opt'), pairs)  17.3 us
    pallas_call x5, Pallas kernels, product(): pl.pallas_call(functools.partial(product_kernel, first=first), in_specs=[...  13.5 us
    ppermute x9, starting transfers between devices, shift(): return lax.ppermute(x, ('dp', 'opt'), pairs)  12.4 us
    convert_element_type x7, other arithmetic, pack(): return x.astype(jnp.float16)  9.56 us
    pallas_call x3, Pallas kernels, dispatch(): pl.pallas_call(functools.partial(dispatch_kernel, blocks=blocks), in_spec...  6.28 us
    unnamed x22, local copies, waits for them, and re-layouts  5.15 us
  transfers between devices with their start and end apart: 13, of which 7 were waited for; matrix products, arithmetic and copies ran while one was open for 12% of the time, Pallas kernels for 19%

profile of v3, /device:TPU:2, one launch (start us, length us, event | category | flops | bytes accessed | tf_op | source)
XLA Modules:
  0.0 117.7 jit_solution(8163387482279197817)
XLA Ops:
  0.7 3.4 %dispatch.3 = bf16[1024,640]{1,0:T(8,128)(2,1)} custom-call(s32[8,256]{1,0:T(8,128)} %bitcast.25, bf16[256,4096]{1,0:T(8,128)(2,1)} %tokens_ref.5), custom_call_target="tpu_custom_call" | custom-call | flops 335544320 | bytes 1966080 | tf_op jit(solution)/shard_map/dispatch/pallas_call | solution.py:81
  4.2 7.8 %all-to-all-start = ((bf16[32,32,640]{2,1,0:T(8,128)(2,1)}), bf16[32,32,640]{2,1,0:T(8,128)(2,1)}, u32[]{:S(2)}, u32[]{:S(2)}) async-start(bf16[32,32,640]{2,1,0:T(8,128)(2,1)} %bitcast.30), calls=%async_computation | async-start | bytes 2621440 | tf_op jit(solution)/shard_map/all_to_all | solution.py:229
  12.0 1.4 %copy-done.6 = bf16[1,1,1,512,1536]{4,3,2,1,0:T(8,128)(2,1)S(1)} copy-done((bf16[1,1,1,512,1536]{4,3,2,1,0:T(8,128)(2,1)S(1)}, bf16[1,1,1,512,1536]{4,3,2,1,0:T(8,128)(2,1)}, u32[]{:S(2)}) %copy-start.6) | copy-done | bytes 1572888
  13.5 1.5 %copy-done = bf16[256,4096]{1,0:T(8,128)(2,1)S(1)} copy-done((bf16[256,4096]{1,0:T(8,128)(2,1)S(1)}, bf16[256,4096]{1,0:T(8,128)(2,1)}, u32[]{:S(2)}) %copy-start) | copy-done | bytes 2097176
  15.0 1.8 %dispatch.4 = bf16[1024,896]{1,0:T(8,128)(2,1)S(1)} custom-call(s32[8,256]{1,0:T(8,128)S(1)} %bitcast.26, bf16[256,4096]{1,0:T(8,128)(2,1)S(1)} %copy-done), custom_call_target="tpu_custom_call" | custom-call | flops 469762048 | bytes 2752512 | tf_op jit(solution)/shard_map/dispatch/pallas_call | solution.py:81
  16.8 1.2 %copy-done.1 = bf16[1024,896]{1,0:T(8,128)(2,1)} copy-done((bf16[1024,896]{1,0:T(8,128)(2,1)}, bf16[1024,896]{1,0:T(8,128)(2,1)S(1)}, u32[]{:S(2)}) %copy-start.1) | copy-done | bytes 1835032
  20.0 11.7 %all-to-all-done = bf16[32,32,640]{2,1,0:T(8,128)(2,1)} async-done(((bf16[32,32,640]{2,1,0:T(8,128)(2,1)}), bf16[32,32,640]{2,1,0:T(8,128)(2,1)}, u32[]{:S(2)}, u32[]{:S(2)}) %all-to-all-start) | async-done | bytes 1310752 | tf_op jit(solution)/shard_map/all_to_all | solution.py:229
  31.7 5.2 %all-to-all-start.1 = ((bf16[32,32,896]{2,1,0:T(8,128)(2,1)}), bf16[32,32,896]{2,1,0:T(8,128)(2,1)}, u32[]{:S(2)}, u32[]{:S(2)}) async-start(bf16[32,32,896]{2,1,0:T(8,128)(2,1)} %bitcast.15), calls=%async_computation.1 | async-start | bytes 3670016 | tf_op jit(solution)/shard_map/all_to_all | solution.py:229
  36.8 3.1 %product.5 = f32[512,1536]{1,0:T(8,128)S(1)} custom-call(bf16[2,512,640]{2,1,0:T(8,128)(2,1)} %bitcast.6.arrived_ref, bf16[512,1536]{1,0:T(8,128)(2,1)S(1)} %hold.1.g_mine, bf16[512,1536]{1,0:T(8,128)(2,1)S(1)} %collective-permute-done.g_other), custom_call_target="tpu_custom_call" | custom-call | flops 1610612736 | bytes 7340032 | tf_op jit(solution)/shard_map/product/pallas_call | solution.py:145
  40.2 1.2 fusion.5
  41.3 1.9 %collective-permute-start.1 = (f16[256,1536]{1,0:T(8,128)(2,1)S(1)}, f16[256,1536]{1,0:T(8,128)(2,1)S(1)}, u32[]{:S(2)}, u32[]{:S(2)}) collective-permute-start(f16[256,1536]{1,0:T(8,128)(2,1)S(1)} %get-tuple-element.51), channel_id=1, source_target_pairs={{0,32},{1,225},{32,64},{33,1},{64,96},{65,33},{96,128},{97,65},{12... | collective-permute-start | bytes 2359304 | tf_op jit(solution)/shard_map/ppermute | solution.py:242
  43.3 1.9 %collective-permute-start.2 = (f16[256,1536]{1,0:T(8,128)(2,1)}, f16[256,1536]{1,0:T(8,128)(2,1)}, u32[]{:S(2)}, u32[]{:S(2)}) collective-permute-start(f16[256,1536]{1,0:T(8,128)(2,1)} %get-tuple-element.52), channel_id=1, source_target_pairs={{0,32},{1,225},{32,64},{33,1},{64,96},{65,33},{96,128},{97,65},{12... | collective-permute-start | bytes 2359304 | tf_op jit(solution)/shard_map/ppermute | solution.py:242
  45.2 1.6 %product.6 = f32[128,1536]{1,0:T(8,128)S(1)} custom-call(bf16[2,512,640]{2,1,0:T(8,128)(2,1)} %bitcast.6.arrived_ref, bf16[512,1536]{1,0:T(8,128)(2,1)S(1)} %hold.1.g_mine, bf16[512,1536]{1,0:T(8,128)(2,1)S(1)} %collective-permute-done.g_other), custom_call_target="tpu_custom_call" | custom-call | flops 402653184 | bytes 4194304 | tf_op jit(solution)/shard_map/product/pallas_call | solution.py:145
  46.8 10.4 %collective-permute-done.1 = f16[256,1536]{1,0:T(8,128)(2,1)S(1)} collective-permute-done((f16[256,1536]{1,0:T(8,128)(2,1)S(1)}, f16[256,1536]{1,0:T(8,128)(2,1)S(1)}, u32[]{:S(2)}, u32[]{:S(2)}) %collective-permute-start.1) | collective-permute-done | bytes 786464 | tf_op jit(solution)/shard_map/ppermute | solution.py:242
  58.2 4.8 %all-to-all-done.1 = bf16[32,32,896]{2,1,0:T(8,128)(2,1)} async-done(((bf16[32,32,896]{2,1,0:T(8,128)(2,1)}), bf16[32,32,896]{2,1,0:T(8,128)(2,1)}, u32[]{:S(2)}, u32[]{:S(2)}) %all-to-all-start.1) | async-done | bytes 1835040 | tf_op jit(solution)/shard_map/all_to_all | solution.py:229
  63.0 2.7 %product.7 = f32[384,1536]{1,0:T(8,128)S(1)} custom-call(bf16[2,512,896]{2,1,0:T(8,128)(2,1)} %bitcast.9.arrived_ref, bf16[512,1536]{1,0:T(8,128)(2,1)S(1)} %hold.1.g_mine, bf16[512,1536]{1,0:T(8,128)(2,1)S(1)} %collective-permute-done.g_other), custom_call_target="tpu_custom_call" | custom-call | flops 1207959552 | bytes 6291456 | tf_op jit(solution)/shard_map/product/pallas_call | solution.py:145
  66.5 1.9 %collective-permute-start.5 = (f16[128,1536]{1,0:T(8,128)(2,1)}, f16[128,1536]{1,0:T(8,128)(2,1)}, u32[]{:S(2)}, u32[]{:S(2)}) collective-permute-start(f16[128,1536]{1,0:T(8,128)(2,1)} %fusion.4), channel_id=1, source_target_pairs={{0,32},{1,225},{32,64},{33,1},{64,96},{65,33},{96,128},{97,65},{12... | collective-permute-start | bytes 1179656 | tf_op jit(solution)/shard_map/ppermute | solution.py:242
  68.5 2.2 %fusion.1 = f16[256,1536]{1,0:T(8,128)(2,1)} fusion(f32[384,1536]{1,0:T(8,128)S(1)} %product.7, f16[256,1536]{1,0:T(8,128)(2,1)} %collective-permute-done.2), kind=kLoop, calls=%fused_computation.4 | loop fusion | flops 1179648 | bytes 3145728 | tf_op jit(solution)/shard_map/convert_element_type | solution.py:239
  70.7 1.9 %collective-permute-start.3 = (f16[256,1536]{1,0:T(8,128)(2,1)}, f16[256,1536]{1,0:T(8,128)(2,1)}, u32[]{:S(2)}, u32[]{:S(2)}) collective-permute-start(f16[256,1536]{1,0:T(8,128)(2,1)} %fusion.1), channel_id=1, source_target_pairs={{0,32},{1,225},{32,64},{33,1},{64,96},{65,33},{96,128},{97,65},{12... | collective-permute-start | bytes 2359304 | tf_op jit(solution)/shard_map/ppermute | solution.py:242
  72.6 6.8 %all-to-all-start.2 = ((bf16[32,32,512]{2,1,0:T(8,128)(2,1)}), bf16[32,32,512]{2,1,0:T(8,128)(2,1)}, u32[]{:S(2)}, u32[]{:S(2)}) async-start(bf16[32,32,512]{2,1,0:T(8,128)(2,1)} %bitcast.22), calls=%async_computation.2 | async-start | bytes 2097152 | tf_op jit(solution)/shard_map/all_to_all | solution.py:229
  79.4 3.1 %product.8 = f32[512,1536]{1,0:T(8,128)S(1)} custom-call(bf16[2,512,896]{2,1,0:T(8,128)(2,1)} %bitcast.9.arrived_ref, bf16[512,1536]{1,0:T(8,128)(2,1)S(1)} %hold.1.g_mine, bf16[512,1536]{1,0:T(8,128)(2,1)S(1)} %collective-permute-done.g_other), custom_call_target="tpu_custom_call" | custom-call | flops 1610612736 | bytes 7340032 | tf_op jit(solution)/shard_map/product/pallas_call | solution.py:145
  82.5 1.2 %pad_maximum_fusion = f16[256,1536]{1,0:T(8,128)(2,1)S(1)} fusion(f16[128,1536]{1,0:T(8,128)(2,1)} %collective-permute-done.5, f16[128,1536]{1,0:T(8,128)(2,1)S(1)} %collective-permute-done.4), kind=kLoop, calls=%fused_computation.12 | loop fusion | flops 393216 | bytes 1572864 | tf_op jit(solution)/shard_map/concatenate | solution.py:266
  83.7 1.1 add_convert_fusion
  86.9 2.2 %fusion = f16[256,1536]{1,0:T(8,128)(2,1)} fusion(f32[512,1536]{1,0:T(8,128)S(1)} %product.8, f16[256,1536]{1,0:T(8,128)(2,1)} %collective-permute-done.3), kind=kLoop, calls=%fused_computation.2 | loop fusion | flops 1179648 | bytes 3145728 | tf_op jit(solution)/shard_map/convert_element_type | solution.py:239
  89.1 7.0 %all-to-all-done.2 = bf16[32,32,512]{2,1,0:T(8,128)(2,1)} async-done(((bf16[32,32,512]{2,1,0:T(8,128)(2,1)}), bf16[32,32,512]{2,1,0:T(8,128)(2,1)}, u32[]{:S(2)}, u32[]{:S(2)}) %all-to-all-start.2) | async-done | bytes 1048608 | tf_op jit(solution)/shard_map/all_to_all | solution.py:229
  96.1 3.1 %product.9 = f32[512,1536]{1,0:T(8,128)S(1)} custom-call(bf16[2,512,512]{2,1,0:T(8,128)(2,1)} %bitcast.11.arrived_ref, bf16[512,1536]{1,0:T(8,128)(2,1)S(1)} %hold.1.g_mine, bf16[512,1536]{1,0:T(8,128)(2,1)S(1)} %collective-permute-done.g_other), custom_call_target="tpu_custom_call" | custom-call | flops 1610612736 | bytes 7340032 | tf_op jit(solution)/shard_map/product/pallas_call | solution.py:145
  102.6 2.6 %collective-permute-start.8 = (f16[256,768]{1,0:T(8,128)(2,1)S(1)}, f16[256,768]{1,0:T(8,128)(2,1)S(1)}, u32[]{:S(2)}, u32[]{:S(2)}) collective-permute-start(f16[256,768]{1,0:T(8,128)(2,1)S(1)} %fusion.3), channel_id=1, source_target_pairs={{0,32},{1,225},{32,64},{33,1},{64,96},{65,33},{96,128},{97,65},{12... | collective-permute-start | bytes 1179656 | tf_op jit(solution)/shard_map/ppermute | solution.py:242
  105.2 1.5 %slice_add_fusion.base = f32[256,1536]{1,0:T(8,128)S(1)} fusion(f32[512,1536]{1,0:T(8,128)S(1)} %product.9, f16[256,1536]{1,0:T(8,128)(2,1)} %collective-permute-done.6), kind=kLoop, calls=%fused_computation | loop fusion | flops 786432 | bytes 3932160 | tf_op jit(solution)/shard_map/add | solution.py:236
  106.7 4.2 %collective-permute-done.9 = f16[256,768]{1,0:T(8,128)(2,1)S(1)} collective-permute-done((f16[256,768]{1,0:T(8,128)(2,1)S(1)}, f16[256,768]{1,0:T(8,128)(2,1)S(1)}, u32[]{:S(2)}, u32[]{:S(2)}) %collective-permute-start.9) | collective-permute-done | bytes 393248 | tf_op jit(solution)/shard_map/ppermute | solution.py:242
  111.0 2.5 %update.2 = (f32[256,1536]{1,0:T(8,128)}, f32[256,1536]{1,0:T(8,128)}, f32[256,1536]{1,0:T(8,128)}) custom-call(s32[2,12]{1,0:T(2,128)S(1)} %bitcast.28, f32[256,1536]{1,0:T(8,128)S(1)} %bitcast.16, f32[256,1536]{1,0:T(8,128)S(1)} %bitcast.18, f32[256,1536]{1,0:T(8,128)S(1)} %bitcast.20, f32[256,1536]{1,0:T(8,128)S(1)} %slice_add_fusion.base, ...), custom_call_target="tpu_custom_call" | custom-call | flops 3932160 | bytes 5505024 | tf_op jit(solution)/shard_map/update/pallas_call | solution.py:193
  113.5 1.6 %collective-permute-done.8 = f16[256,768]{1,0:T(8,128)(2,1)S(1)} collective-permute-done((f16[256,768]{1,0:T(8,128)(2,1)S(1)}, f16[256,768]{1,0:T(8,128)(2,1)S(1)}, u32[]{:S(2)}, u32[]{:S(2)}) %collective-permute-start.8) | collective-permute-done | bytes 393248 | tf_op jit(solution)/shard_map/ppermute | solution.py:242
  115.2 2.5 %update.3 = (f32[256,1536]{1,0:T(8,128)}, f32[256,1536]{1,0:T(8,128)}, f32[256,1536]{1,0:T(8,128)}) custom-call(s32[2,12]{1,0:T(2,128)S(1)} %bitcast.29, f32[256,1536]{1,0:T(8,128)S(1)} %bitcast.17, f32[256,1536]{1,0:T(8,128)S(1)} %bitcast.19, f32[256,1536]{1,0:T(8,128)S(1)} %bitcast.21, ...), custom_call_target="tpu_custom_call", output_to_operand_aliasing={{0}: (6, {}), {1}: (7, {}), {2}: (8, {})} | custom-call | flops 3932160 | bytes 5505024 | tf_op jit(solution)/shard_map/update/pallas_call | solution.py:193
  (40 shorter events, 9.7 us)
Async XLA Ops:
  0.6 31.1 %collective-permute-start = (bf16[512,1536]{1,0:T(8,128)(2,1)}, bf16[512,1536]{1,0:T(8,128)(2,1)S(1)}, u32[]{:S(2)}, u32[]{:S(2)}) collective-permute-start(bf16[512,1536]{1,0:T(8,128)(2,1)} %bitcast.23), channel_id=1, source_target_pairs={{0,1},{1,0},{2,3},{3,2},{4,5},{5,4},{6,7},{7,6},{8,9},{9,8},{10,11... | collective-permute-start | bytes 4718600 | tf_op jit(solution)/shard_map/ppermute | solution.py:218
  4.2 27.5 %all-to-all-start = ((bf16[32,32,640]{2,1,0:T(8,128)(2,1)}), bf16[32,32,640]{2,1,0:T(8,128)(2,1)}, u32[]{:S(2)}, u32[]{:S(2)}) async-start(bf16[32,32,640]{2,1,0:T(8,128)(2,1)} %bitcast.30), calls=%async_computation | async-start | bytes 2621440 | tf_op jit(solution)/shard_map/all_to_all | solution.py:229
  12.0 1.4 %copy-start.6 = (bf16[1,1,1,512,1536]{4,3,2,1,0:T(8,128)(2,1)S(1)}, bf16[1,1,1,512,1536]{4,3,2,1,0:T(8,128)(2,1)}, u32[]{:S(2)}) copy-start(bf16[1,1,1,512,1536]{4,3,2,1,0:T(8,128)(2,1)} %param.9) | copy-start | bytes 4718596
  13.4 1.6 %copy-start = (bf16[256,4096]{1,0:T(8,128)(2,1)S(1)}, bf16[256,4096]{1,0:T(8,128)(2,1)}, u32[]{:S(2)}) copy-start(bf16[256,4096]{1,0:T(8,128)(2,1)} %tokens_ref.5) | copy-start | bytes 6291460
  13.4 1.6 %copy-start.7 = (s32[256,8]{0,1:T(8,128)S(1)}, s32[256,8]{0,1:T(8,128)}, u32[]{:S(2)}) copy-start(s32[256,8]{0,1:T(8,128)} %param.8) | copy-start | bytes 24580
  16.8 1.2 %copy-start.1 = (bf16[1024,896]{1,0:T(8,128)(2,1)}, bf16[1024,896]{1,0:T(8,128)(2,1)S(1)}, u32[]{:S(2)}) copy-start(bf16[1024,896]{1,0:T(8,128)(2,1)S(1)} %dispatch.4) | copy-start | bytes 5505028
  19.0 1.0 copy-start.5
  31.7 31.3 %all-to-all-start.1 = ((bf16[32,32,896]{2,1,0:T(8,128)(2,1)}), bf16[32,32,896]{2,1,0:T(8,128)(2,1)}, u32[]{:S(2)}, u32[]{:S(2)}) async-start(bf16[32,32,896]{2,1,0:T(8,128)(2,1)} %bitcast.15), calls=%async_computation.1 | async-start | bytes 3670016 | tf_op jit(solution)/shard_map/all_to_all | solution.py:229
  41.3 15.8 %collective-permute-start.1 = (f16[256,1536]{1,0:T(8,128)(2,1)S(1)}, f16[256,1536]{1,0:T(8,128)(2,1)S(1)}, u32[]{:S(2)}, u32[]{:S(2)}) collective-permute-start(f16[256,1536]{1,0:T(8,128)(2,1)S(1)} %get-tuple-element.51), channel_id=1, source_target_pairs={{0,32},{1,225},{32,64},{33,1},{64,96},{65,33},{96,128},{97,65},{12... | collective-permute-start | bytes 2359304 | tf_op jit(solution)/shard_map/ppermute | solution.py:242
  43.3 25.2 %collective-permute-start.2 = (f16[256,1536]{1,0:T(8,128)(2,1)}, f16[256,1536]{1,0:T(8,128)(2,1)}, u32[]{:S(2)}, u32[]{:S(2)}) collective-permute-start(f16[256,1536]{1,0:T(8,128)(2,1)} %get-tuple-element.52), channel_id=1, source_target_pairs={{0,32},{1,225},{32,64},{33,1},{64,96},{65,33},{96,128},{97,65},{12... | collective-permute-start | bytes 2359304 | tf_op jit(solution)/shard_map/ppermute | solution.py:242
  57.2 1.0 copy-start.9
  58.2 24.3 %collective-permute-start.4 = (f16[128,1536]{1,0:T(8,128)(2,1)}, f16[128,1536]{1,0:T(8,128)(2,1)S(1)}, u32[]{:S(2)}, u32[]{:S(2)}) collective-permute-start(f16[128,1536]{1,0:T(8,128)(2,1)} %add_convert_fusion.1), channel_id=1, source_target_pairs={{0,32},{1,225},{32,64},{33,1},{64,96},{65,33},{96,128},{97,65},{12... | collective-permute-start | bytes 1179656 | tf_op jit(solution)/shard_map/ppermute | solution.py:242
  63.0 2.7 %copy-start.10 = (f16[256,1536]{1,0:T(8,128)(2,1)S(1)}, f16[256,1536]{1,0:T(8,128)(2,1)}, u32[]{:S(2)}) copy-start(f16[256,1536]{1,0:T(8,128)(2,1)} %copy-done.9) | copy-start | bytes 2359300
  66.5 16.0 %collective-permute-start.5 = (f16[128,1536]{1,0:T(8,128)(2,1)}, f16[128,1536]{1,0:T(8,128)(2,1)}, u32[]{:S(2)}, u32[]{:S(2)}) collective-permute-start(f16[128,1536]{1,0:T(8,128)(2,1)} %fusion.4), channel_id=1, source_target_pairs={{0,32},{1,225},{32,64},{33,1},{64,96},{65,33},{96,128},{97,65},{12... | collective-permute-start | bytes 1179656 | tf_op jit(solution)/shard_map/ppermute | solution.py:242
  70.7 16.2 %collective-permute-start.3 = (f16[256,1536]{1,0:T(8,128)(2,1)}, f16[256,1536]{1,0:T(8,128)(2,1)}, u32[]{:S(2)}, u32[]{:S(2)}) collective-permute-start(f16[256,1536]{1,0:T(8,128)(2,1)} %fusion.1), channel_id=1, source_target_pairs={{0,32},{1,225},{32,64},{33,1},{64,96},{65,33},{96,128},{97,65},{12... | collective-permute-start | bytes 2359304 | tf_op jit(solution)/shard_map/ppermute | solution.py:242
  72.6 23.6 %all-to-all-start.2 = ((bf16[32,32,512]{2,1,0:T(8,128)(2,1)}), bf16[32,32,512]{2,1,0:T(8,128)(2,1)}, u32[]{:S(2)}, u32[]{:S(2)}) async-start(bf16[32,32,512]{2,1,0:T(8,128)(2,1)} %bitcast.22), calls=%async_computation.2 | async-start | bytes 2097152 | tf_op jit(solution)/shard_map/all_to_all | solution.py:229
  84.9 14.4 %collective-permute-start.7 = (f16[256,1536]{1,0:T(8,128)(2,1)}, f16[256,1536]{1,0:T(8,128)(2,1)}, u32[]{:S(2)}, u32[]{:S(2)}) collective-permute-start(f16[256,1536]{1,0:T(8,128)(2,1)} %add_convert_fusion), channel_id=1, source_target_pairs={{0,32},{1,225},{32,64},{33,1},{64,96},{65,33},{96,128},{97,65},{12... | collective-permute-start | bytes 2359304 | tf_op jit(solution)/shard_map/ppermute | solution.py:242
  89.1 16.1 %collective-permute-start.6 = (f16[256,1536]{1,0:T(8,128)(2,1)}, f16[256,1536]{1,0:T(8,128)(2,1)}, u32[]{:S(2)}, u32[]{:S(2)}) collective-permute-start(f16[256,1536]{1,0:T(8,128)(2,1)} %fusion), channel_id=1, source_target_pairs={{0,33},{1,224},{32,65},{33,0},{64,97},{65,32},{96,129},{97,64},{12... | collective-permute-start | bytes 2359304 | tf_op jit(solution)/shard_map/ppermute | solution.py:242
  100.4 10.5 %collective-permute-start.9 = (f16[256,768]{1,0:T(8,128)(2,1)S(1)}, f16[256,768]{1,0:T(8,128)(2,1)S(1)}, u32[]{:S(2)}, u32[]{:S(2)}) collective-permute-start(f16[256,768]{1,0:T(8,128)(2,1)S(1)} %fusion.2), channel_id=1, source_target_pairs={{0,32},{1,225},{32,64},{33,1},{64,96},{65,33},{96,128},{97,65},{12... | collective-permute-start | bytes 1179656 | tf_op jit(solution)/shard_map/ppermute | solution.py:242
  102.5 8.4 %copy-start.8 = (s32[1,2,12]{2,1,0:T(2,128)S(1)}, s32[1,2,12]{2,1,0:T(2,128)}, u32[]{:S(2)}) copy-start(s32[1,2,12]{2,1,0:T(2,128)} %param.10) | copy-start | bytes 292
  102.6 12.6 %collective-permute-start.8 = (f16[256,768]{1,0:T(8,128)(2,1)S(1)}, f16[256,768]{1,0:T(8,128)(2,1)S(1)}, u32[]{:S(2)}, u32[]{:S(2)}) collective-permute-start(f16[256,768]{1,0:T(8,128)(2,1)S(1)} %fusion.3), channel_id=1, source_target_pairs={{0,32},{1,225},{32,64},{33,1},{64,96},{65,33},{96,128},{97,65},{12... | collective-permute-start | bytes 1179656 | tf_op jit(solution)/shard_map/ppermute | solution.py:242
  105.2 5.8 %copy-start.2 = (f32[1,256,1536]{2,1,0:T(8,128)S(1)}, f32[1,256,1536]{2,1,0:T(8,128)}, u32[]{:S(2)}) copy-start(f32[1,256,1536]{2,1,0:T(8,128)} %param.11) | copy-start | bytes 4718596
  105.2 5.8 %copy-start.3 = (f32[1,256,1536]{2,1,0:T(8,128)S(1)}, f32[1,256,1536]{2,1,0:T(8,128)}, u32[]{:S(2)}) copy-start(f32[1,256,1536]{2,1,0:T(8,128)} %param.12) | copy-start | bytes 4718596
  105.2 5.8 %copy-start.4 = (f32[1,256,1536]{2,1,0:T(8,128)S(1)}, f32[1,256,1536]{2,1,0:T(8,128)}, u32[]{:S(2)}) copy-start(f32[1,256,1536]{2,1,0:T(8,128)} %param.13) | copy-start | bytes 4718596

commit v4 on v3

--- a/solution.py
+++ b/solution.py
@@ -262,10 +262,11 @@
     far_out = pack(plus(two_b, after(far, near_out)))
     far = shift(far_out, ahead)
     last = exchange(after(sent_3, far_out))
-    two_a, one_b = totals(after(late, far_out), some + HALF, HALF, HALF)
+    (two_a,) = totals(after(late, far_out), some + HALF, HALF)
     near = after(jnp.concatenate([near_1, near_2]), two_a)
     near_out = pack(plus(two_a, near))
     near = shift(near_out, ahead)
+    (one_b,) = totals(after(late, near_out), some + 2 * HALF, HALF)
     far_out = pack(plus(one_b, after(far, near_out)))
     far = shift(far_out, across)
     one_a, own = totals(after(last, far_out), 0, HALF, HALF)

time: 118 us -> 118 us (level)
  waiting for transfers between devices: 40.8 us -> 38.1 us
    ppermute x9, waiting for transfers between devices: 17.3 us -> 15.1 us  [shift(): return lax.ppermute(x, ('dp', 'opt'), pairs)]
    pallas_call x5 -> x6, Pallas kernels: 13.5 us -> 14.6 us  [product(): pl.pallas_call(functools.partial(product_kernel, first=first), in_specs=[...]
  transfers between devices with their start and end apart: 13 -> 13, of which waited for: 7 -> 6; matrix products, arithmetic and copies ran while one was open for 12% -> 12% of each run, Pallas kernels for 19% -> 20%
where the time goes in v4:
time: 118 us; the launch traced here: 117 us
  waiting for transfers between devices  38.1 us (32%)
  starting transfers between devices  32.7 us (28%)
  Pallas kernels  26 us (22%)
  other arithmetic  12.6 us (11%)
  local copies, waits for them, and re-layouts  6.32 us (5%)
    all_to_all x3, waiting for transfers between devices, exchange(): lax.all_to_all(sent, ('opt', 'expert'), 0, 0, tiled=True)  23 us
    all_to_all x3, starting transfers between devices, exchange(): lax.all_to_all(sent, ('opt', 'expert'), 0, 0, tiled=True)  19.8 us
    ppermute x9, waiting for transfers between devices, shift(): return lax.ppermute(x, ('dp', 'opt'), pairs)  15.1 us
    pallas_call x6, Pallas kernels, product(): pl.pallas_call(functools.partial(product_kernel, first=first), in_specs=[...  14.6 us
    ppermute x9, starting transfers between devices, shift(): return lax.ppermute(x, ('dp', 'opt'), pairs)  12.9 us
    convert_element_type x7, other arithmetic, pack(): return x.astype(jnp.float16)  9.61 us
    pallas_call x3, Pallas kernels, dispatch(): pl.pallas_call(functools.partial(dispatch_kernel, blocks=blocks), in_spec...  6.28 us
    unnamed x22, local copies, waits for them, and re-layouts  5.15 us
  transfers between devices with their start and end apart: 13, of which 6 were waited for; matrix products, arithmetic and copies ran while one was open for 12% of the time, Pallas kernels for 20%

profile of v4, /device:TPU:2, one launch (start us, length us, event | category | flops | bytes accessed | tf_op | source)
XLA Modules:
  0.0 116.7 jit_solution(4678298524940714164)
XLA Ops:
  0.7 3.4 %dispatch.3 = bf16[1024,640]{1,0:T(8,128)(2,1)} custom-call(s32[8,256]{1,0:T(8,128)} %bitcast.25, bf16[256,4096]{1,0:T(8,128)(2,1)} %tokens_ref.5), custom_call_target="tpu_custom_call" | custom-call | flops 335544320 | bytes 1966080 | tf_op jit(solution)/shard_map/dispatch/pallas_call | solution.py:81
  4.2 7.8 %all-to-all-start = ((bf16[32,32,640]{2,1,0:T(8,128)(2,1)}), bf16[32,32,640]{2,1,0:T(8,128)(2,1)}, u32[]{:S(2)}, u32[]{:S(2)}) async-start(bf16[32,32,640]{2,1,0:T(8,128)(2,1)} %bitcast.30), calls=%async_computation | async-start | bytes 2621440 | tf_op jit(solution)/shard_map/all_to_all | solution.py:229
  12.0 1.4 %copy-done.6 = bf16[1,1,1,512,1536]{4,3,2,1,0:T(8,128)(2,1)S(1)} copy-done((bf16[1,1,1,512,1536]{4,3,2,1,0:T(8,128)(2,1)S(1)}, bf16[1,1,1,512,1536]{4,3,2,1,0:T(8,128)(2,1)}, u32[]{:S(2)}) %copy-start.6) | copy-done | bytes 1572888
  13.5 1.5 %copy-done = bf16[256,4096]{1,0:T(8,128)(2,1)S(1)} copy-done((bf16[256,4096]{1,0:T(8,128)(2,1)S(1)}, bf16[256,4096]{1,0:T(8,128)(2,1)}, u32[]{:S(2)}) %copy-start) | copy-done | bytes 2097176
  15.0 1.8 %dispatch.4 = bf16[1024,896]{1,0:T(8,128)(2,1)S(1)} custom-call(s32[8,256]{1,0:T(8,128)S(1)} %bitcast.26, bf16[256,4096]{1,0:T(8,128)(2,1)S(1)} %copy-done), custom_call_target="tpu_custom_call" | custom-call | flops 469762048 | bytes 2752512 | tf_op jit(solution)/shard_map/dispatch/pallas_call | solution.py:81
  16.8 1.2 %copy-done.1 = bf16[1024,896]{1,0:T(8,128)(2,1)} copy-done((bf16[1024,896]{1,0:T(8,128)(2,1)}, bf16[1024,896]{1,0:T(8,128)(2,1)S(1)}, u32[]{:S(2)}) %copy-start.1) | copy-done | bytes 1835032
  20.0 11.7 %all-to-all-done = bf16[32,32,640]{2,1,0:T(8,128)(2,1)} async-done(((bf16[32,32,640]{2,1,0:T(8,128)(2,1)}), bf16[32,32,640]{2,1,0:T(8,128)(2,1)}, u32[]{:S(2)}, u32[]{:S(2)}) %all-to-all-start) | async-done | bytes 1310752 | tf_op jit(solution)/shard_map/all_to_all | solution.py:229
  31.7 5.2 %all-to-all-start.1 = ((bf16[32,32,896]{2,1,0:T(8,128)(2,1)}), bf16[32,32,896]{2,1,0:T(8,128)(2,1)}, u32[]{:S(2)}, u32[]{:S(2)}) async-start(bf16[32,32,896]{2,1,0:T(8,128)(2,1)} %bitcast.15), calls=%async_computation.1 | async-start | bytes 3670016 | tf_op jit(solution)/shard_map/all_to_all | solution.py:229
  36.8 3.1 %product.6 = f32[512,1536]{1,0:T(8,128)S(1)} custom-call(bf16[2,512,640]{2,1,0:T(8,128)(2,1)} %bitcast.6.arrived_ref, bf16[512,1536]{1,0:T(8,128)(2,1)S(1)} %hold.1.g_mine, bf16[512,1536]{1,0:T(8,128)(2,1)S(1)} %collective-permute-done.g_other), custom_call_target="tpu_custom_call" | custom-call | flops 1610612736 | bytes 7340032 | tf_op jit(solution)/shard_map/product/pallas_call | solution.py:145
  40.2 1.2 %fusion.4 = (f16[256,1536]{1,0:T(8,128)(2,1)S(1)}, f16[256,1536]{1,0:T(8,128)(2,1)}) fusion(f16[512,1536]{1,0:T(8,128)(2,1)S(1)} %convert.4), kind=kLoop, calls=%fused_computation.13 | loop fusion | bytes 3145728 | tf_op jit(solution)/shard_map/split | solution.py:233
  41.3 1.9 %collective-permute-start.1 = (f16[256,1536]{1,0:T(8,128)(2,1)S(1)}, f16[256,1536]{1,0:T(8,128)(2,1)S(1)}, u32[]{:S(2)}, u32[]{:S(2)}) collective-permute-start(f16[256,1536]{1,0:T(8,128)(2,1)S(1)} %get-tuple-element.53), channel_id=1, source_target_pairs={{0,32},{1,225},{32,64},{33,1},{64,96},{65,33},{96,128},{97,65},{12... | collective-permute-start | bytes 2359304 | tf_op jit(solution)/shard_map/ppermute | solution.py:242
  43.3 1.9 %collective-permute-start.2 = (f16[256,1536]{1,0:T(8,128)(2,1)}, f16[256,1536]{1,0:T(8,128)(2,1)}, u32[]{:S(2)}, u32[]{:S(2)}) collective-permute-start(f16[256,1536]{1,0:T(8,128)(2,1)} %get-tuple-element.54), channel_id=1, source_target_pairs={{0,32},{1,225},{32,64},{33,1},{64,96},{65,33},{96,128},{97,65},{12... | collective-permute-start | bytes 2359304 | tf_op jit(solution)/shard_map/ppermute | solution.py:242
  45.2 1.6 %product.7 = f32[128,1536]{1,0:T(8,128)S(1)} custom-call(bf16[2,512,640]{2,1,0:T(8,128)(2,1)} %bitcast.6.arrived_ref, bf16[512,1536]{1,0:T(8,128)(2,1)S(1)} %hold.1.g_mine, bf16[512,1536]{1,0:T(8,128)(2,1)S(1)} %collective-permute-done.g_other), custom_call_target="tpu_custom_call" | custom-call | flops 402653184 | bytes 4194304 | tf_op jit(solution)/shard_map/product/pallas_call | solution.py:145
  46.8 10.4 %collective-permute-done.1 = f16[256,1536]{1,0:T(8,128)(2,1)S(1)} collective-permute-done((f16[256,1536]{1,0:T(8,128)(2,1)S(1)}, f16[256,1536]{1,0:T(8,128)(2,1)S(1)}, u32[]{:S(2)}, u32[]{:S(2)}) %collective-permute-start.1) | collective-permute-done | bytes 786464 | tf_op jit(solution)/shard_map/ppermute | solution.py:242
  58.2 4.8 %all-to-all-done.1 = bf16[32,32,896]{2,1,0:T(8,128)(2,1)} async-done(((bf16[32,32,896]{2,1,0:T(8,128)(2,1)}), bf16[32,32,896]{2,1,0:T(8,128)(2,1)}, u32[]{:S(2)}, u32[]{:S(2)}) %all-to-all-start.1) | async-done | bytes 1835040 | tf_op jit(solution)/shard_map/all_to_all | solution.py:229
  63.0 2.7 %product.8 = f32[384,1536]{1,0:T(8,128)S(1)} custom-call(bf16[2,512,896]{2,1,0:T(8,128)(2,1)} %bitcast.9.arrived_ref, bf16[512,1536]{1,0:T(8,128)(2,1)S(1)} %hold.1.g_mine, bf16[512,1536]{1,0:T(8,128)(2,1)S(1)} %collective-permute-done.g_other), custom_call_target="tpu_custom_call" | custom-call | flops 1207959552 | bytes 6291456 | tf_op jit(solution)/shard_map/product/pallas_call | solution.py:145
  66.5 1.9 %collective-permute-start.4 = (f16[128,1536]{1,0:T(8,128)(2,1)}, f16[128,1536]{1,0:T(8,128)(2,1)}, u32[]{:S(2)}, u32[]{:S(2)}) collective-permute-start(f16[128,1536]{1,0:T(8,128)(2,1)} %fusion.3), channel_id=1, source_target_pairs={{0,32},{1,225},{32,64},{33,1},{64,96},{65,33},{96,128},{97,65},{12... | collective-permute-start | bytes 1179656 | tf_op jit(solution)/shard_map/ppermute | solution.py:242
  68.5 2.2 %fusion = f16[256,1536]{1,0:T(8,128)(2,1)} fusion(f32[384,1536]{1,0:T(8,128)S(1)} %product.8, f16[256,1536]{1,0:T(8,128)(2,1)} %collective-permute-done.2), kind=kLoop, calls=%fused_computation.2 | loop fusion | flops 1179648 | bytes 3145728 | tf_op jit(solution)/shard_map/convert_element_type | solution.py:239
  70.7 1.9 %collective-permute-start.5 = (f16[256,1536]{1,0:T(8,128)(2,1)}, f16[256,1536]{1,0:T(8,128)(2,1)}, u32[]{:S(2)}, u32[]{:S(2)}) collective-permute-start(f16[256,1536]{1,0:T(8,128)(2,1)} %fusion), channel_id=1, source_target_pairs={{0,32},{1,225},{32,64},{33,1},{64,96},{65,33},{96,128},{97,65},{12... | collective-permute-start | bytes 2359304 | tf_op jit(solution)/shard_map/ppermute | solution.py:242
  72.6 6.8 %all-to-all-start.2 = ((bf16[32,32,512]{2,1,0:T(8,128)(2,1)}), bf16[32,32,512]{2,1,0:T(8,128)(2,1)}, u32[]{:S(2)}, u32[]{:S(2)}) async-start(bf16[32,32,512]{2,1,0:T(8,128)(2,1)} %bitcast.22), calls=%async_computation.2 | async-start | bytes 2097152 | tf_op jit(solution)/shard_map/all_to_all | solution.py:229
  79.4 2.1 %product.9 = f32[256,1536]{1,0:T(8,128)S(1)} custom-call(bf16[2,512,896]{2,1,0:T(8,128)(2,1)} %bitcast.9.arrived_ref, bf16[512,1536]{1,0:T(8,128)(2,1)S(1)} %hold.1.g_mine, bf16[512,1536]{1,0:T(8,128)(2,1)S(1)} %collective-permute-done.g_other), custom_call_target="tpu_custom_call" | custom-call | flops 805306368 | bytes 5242880 | tf_op jit(solution)/shard_map/product/pallas_call | solution.py:145
  81.5 1.2 %pad_maximum_fusion = f16[256,1536]{1,0:T(8,128)(2,1)S(1)} fusion(f16[128,1536]{1,0:T(8,128)(2,1)} %collective-permute-done.4, f16[128,1536]{1,0:T(8,128)(2,1)S(1)} %collective-permute-done.3), kind=kLoop, calls=%fused_computation.11 | loop fusion | flops 393216 | bytes 1572864 | tf_op jit(solution)/shard_map/concatenate | solution.py:266
  84.9 2.1 %product.10 = f32[256,1536]{1,0:T(8,128)S(1)} custom-call(bf16[2,512,896]{2,1,0:T(8,128)(2,1)} %bitcast.9.arrived_ref, bf16[512,1536]{1,0:T(8,128)(2,1)S(1)} %hold.1.g_mine, bf16[512,1536]{1,0:T(8,128)(2,1)S(1)} %collective-permute-done.g_other), custom_call_target="tpu_custom_call" | custom-call | flops 805306368 | bytes 5242880 | tf_op jit(solution)/shard_map/product/pallas_call | solution.py:145
  87.0 2.2 %add_convert_fusion = f16[256,1536]{1,0:T(8,128)(2,1)} fusion(f32[256,1536]{1,0:T(8,128)S(1)} %product.10, f16[256,1536]{1,0:T(8,128)(2,1)} %collective-permute-done.5), kind=kLoop, calls=%fused_computation.3 | loop fusion | flops 1179648 | bytes 3145728 | tf_op jit(solution)/shard_map/convert_element_type | solution.py:239
  89.7 6.5 %all-to-all-done.2 = bf16[32,32,512]{2,1,0:T(8,128)(2,1)} async-done(((bf16[32,32,512]{2,1,0:T(8,128)(2,1)}), bf16[32,32,512]{2,1,0:T(8,128)(2,1)}, u32[]{:S(2)}, u32[]{:S(2)}) %all-to-all-start.2) | async-done | bytes 1048608 | tf_op jit(solution)/shard_map/all_to_all | solution.py:229
  96.1 3.1 %product.11 = f32[512,1536]{1,0:T(8,128)S(1)} custom-call(bf16[2,512,512]{2,1,0:T(8,128)(2,1)} %bitcast.11.arrived_ref, bf16[512,1536]{1,0:T(8,128)(2,1)S(1)} %hold.1.g_mine, bf16[512,1536]{1,0:T(8,128)(2,1)S(1)} %collective-permute-done.g_other), custom_call_target="tpu_custom_call" | custom-call | flops 1610612736 | bytes 7340032 | tf_op jit(solution)/shard_map/product/pallas_call | solution.py:145
  102.6 2.6 %collective-permute-start.8 = (f16[256,768]{1,0:T(8,128)(2,1)S(1)}, f16[256,768]{1,0:T(8,128)(2,1)S(1)}, u32[]{:S(2)}, u32[]{:S(2)}) collective-permute-start(f16[256,768]{1,0:T(8,128)(2,1)S(1)} %fusion.2), channel_id=1, source_target_pairs={{0,32},{1,225},{32,64},{33,1},{64,96},{65,33},{96,128},{97,65},{12... | collective-permute-start | bytes 1179656 | tf_op jit(solution)/shard_map/ppermute | solution.py:242
  105.3 1.5 %slice_add_fusion.base = f32[256,1536]{1,0:T(8,128)S(1)} fusion(f32[512,1536]{1,0:T(8,128)S(1)} %product.11, f16[256,1536]{1,0:T(8,128)(2,1)} %collective-permute-done.6), kind=kLoop, calls=%fused_computation | loop fusion | flops 786432 | bytes 3932160 | tf_op jit(solution)/shard_map/add | solution.py:236
  106.8 3.1 %collective-permute-done.9 = f16[256,768]{1,0:T(8,128)(2,1)S(1)} collective-permute-done((f16[256,768]{1,0:T(8,128)(2,1)S(1)}, f16[256,768]{1,0:T(8,128)(2,1)S(1)}, u32[]{:S(2)}, u32[]{:S(2)}) %collective-permute-start.9) | collective-permute-done | bytes 393248 | tf_op jit(solution)/shard_map/ppermute | solution.py:242
  110.0 2.5 %update.2 = (f32[256,1536]{1,0:T(8,128)}, f32[256,1536]{1,0:T(8,128)}, f32[256,1536]{1,0:T(8,128)}) custom-call(s32[2,12]{1,0:T(2,128)S(1)} %bitcast.28, f32[256,1536]{1,0:T(8,128)S(1)} %bitcast.16, f32[256,1536]{1,0:T(8,128)S(1)} %bitcast.18, f32[256,1536]{1,0:T(8,128)S(1)} %bitcast.20, f32[256,1536]{1,0:T(8,128)S(1)} %slice_add_fusion.base, ...), custom_call_target="tpu_custom_call" | custom-call | flops 3932160 | bytes 5505024 | tf_op jit(solution)/shard_map/update/pallas_call | solution.py:193
  112.5 1.6 %collective-permute-done.8 = f16[256,768]{1,0:T(8,128)(2,1)S(1)} collective-permute-done((f16[256,768]{1,0:T(8,128)(2,1)S(1)}, f16[256,768]{1,0:T(8,128)(2,1)S(1)}, u32[]{:S(2)}, u32[]{:S(2)}) %collective-permute-start.8) | collective-permute-done | bytes 393248 | tf_op jit(solution)/shard_map/ppermute | solution.py:242
  114.2 2.5 %update.3 = (f32[256,1536]{1,0:T(8,128)}, f32[256,1536]{1,0:T(8,128)}, f32[256,1536]{1,0:T(8,128)}) custom-call(s32[2,12]{1,0:T(2,128)S(1)} %bitcast.29, f32[256,1536]{1,0:T(8,128)S(1)} %bitcast.17, f32[256,1536]{1,0:T(8,128)S(1)} %bitcast.19, f32[256,1536]{1,0:T(8,128)S(1)} %bitcast.21, ...), custom_call_target="tpu_custom_call", output_to_operand_aliasing={{0}: (6, {}), {1}: (7, {}), {2}: (8, {})} | custom-call | flops 3932160 | bytes 5505024 | tf_op jit(solution)/shard_map/update/pallas_call | solution.py:193
  (41 shorter events, 10.4 us)
Async XLA Ops:
  0.6 31.1 %collective-permute-start = (bf16[512,1536]{1,0:T(8,128)(2,1)}, bf16[512,1536]{1,0:T(8,128)(2,1)S(1)}, u32[]{:S(2)}, u32[]{:S(2)}) collective-permute-start(bf16[512,1536]{1,0:T(8,128)(2,1)} %bitcast.23), channel_id=1, source_target_pairs={{0,1},{1,0},{2,3},{3,2},{4,5},{5,4},{6,7},{7,6},{8,9},{9,8},{10,11... | collective-permute-start | bytes 4718600 | tf_op jit(solution)/shard_map/ppermute | solution.py:218
  4.2 27.5 %all-to-all-start = ((bf16[32,32,640]{2,1,0:T(8,128)(2,1)}), bf16[32,32,640]{2,1,0:T(8,128)(2,1)}, u32[]{:S(2)}, u32[]{:S(2)}) async-start(bf16[32,32,640]{2,1,0:T(8,128)(2,1)} %bitcast.30), calls=%async_computation | async-start | bytes 2621440 | tf_op jit(solution)/shard_map/all_to_all | solution.py:229
  12.0 1.4 %copy-start.6 = (bf16[1,1,1,512,1536]{4,3,2,1,0:T(8,128)(2,1)S(1)}, bf16[1,1,1,512,1536]{4,3,2,1,0:T(8,128)(2,1)}, u32[]{:S(2)}) copy-start(bf16[1,1,1,512,1536]{4,3,2,1,0:T(8,128)(2,1)} %param.9) | copy-start | bytes 4718596
  13.4 1.6 %copy-start = (bf16[256,4096]{1,0:T(8,128)(2,1)S(1)}, bf16[256,4096]{1,0:T(8,128)(2,1)}, u32[]{:S(2)}) copy-start(bf16[256,4096]{1,0:T(8,128)(2,1)} %tokens_ref.5) | copy-start | bytes 6291460
  13.4 1.6 %copy-start.7 = (s32[256,8]{0,1:T(8,128)S(1)}, s32[256,8]{0,1:T(8,128)}, u32[]{:S(2)}) copy-start(s32[256,8]{0,1:T(8,128)} %param.8) | copy-start | bytes 24580
  16.8 1.2 %copy-start.1 = (bf16[1024,896]{1,0:T(8,128)(2,1)}, bf16[1024,896]{1,0:T(8,128)(2,1)S(1)}, u32[]{:S(2)}) copy-start(bf16[1024,896]{1,0:T(8,128)(2,1)S(1)} %dispatch.4) | copy-start | bytes 5505028
  19.0 1.0 copy-start.5
  31.7 31.3 %all-to-all-start.1 = ((bf16[32,32,896]{2,1,0:T(8,128)(2,1)}), bf16[32,32,896]{2,1,0:T(8,128)(2,1)}, u32[]{:S(2)}, u32[]{:S(2)}) async-start(bf16[32,32,896]{2,1,0:T(8,128)(2,1)} %bitcast.15), calls=%async_computation.1 | async-start | bytes 3670016 | tf_op jit(solution)/shard_map/all_to_all | solution.py:229
  41.3 15.8 %collective-permute-start.1 = (f16[256,1536]{1,0:T(8,128)(2,1)S(1)}, f16[256,1536]{1,0:T(8,128)(2,1)S(1)}, u32[]{:S(2)}, u32[]{:S(2)}) collective-permute-start(f16[256,1536]{1,0:T(8,128)(2,1)S(1)} %get-tuple-element.53), channel_id=1, source_target_pairs={{0,32},{1,225},{32,64},{33,1},{64,96},{65,33},{96,128},{97,65},{12... | collective-permute-start | bytes 2359304 | tf_op jit(solution)/shard_map/ppermute | solution.py:242
  43.3 25.2 %collective-permute-start.2 = (f16[256,1536]{1,0:T(8,128)(2,1)}, f16[256,1536]{1,0:T(8,128)(2,1)}, u32[]{:S(2)}, u32[]{:S(2)}) collective-permute-start(f16[256,1536]{1,0:T(8,128)(2,1)} %get-tuple-element.54), channel_id=1, source_target_pairs={{0,32},{1,225},{32,64},{33,1},{64,96},{65,33},{96,128},{97,65},{12... | collective-permute-start | bytes 2359304 | tf_op jit(solution)/shard_map/ppermute | solution.py:242
  57.2 1.0 copy-start.9
  58.2 23.3 %collective-permute-start.3 = (f16[128,1536]{1,0:T(8,128)(2,1)}, f16[128,1536]{1,0:T(8,128)(2,1)S(1)}, u32[]{:S(2)}, u32[]{:S(2)}) collective-permute-start(f16[128,1536]{1,0:T(8,128)(2,1)} %add_convert_fusion.2), channel_id=1, source_target_pairs={{0,32},{1,225},{32,64},{33,1},{64,96},{65,33},{96,128},{97,65},{12... | collective-permute-start | bytes 1179656 | tf_op jit(solution)/shard_map/ppermute | solution.py:242
  63.0 2.7 %copy-start.10 = (f16[256,1536]{1,0:T(8,128)(2,1)S(1)}, f16[256,1536]{1,0:T(8,128)(2,1)}, u32[]{:S(2)}) copy-start(f16[256,1536]{1,0:T(8,128)(2,1)} %copy-done.9) | copy-start | bytes 2359300
  66.5 15.0 %collective-permute-start.4 = (f16[128,1536]{1,0:T(8,128)(2,1)}, f16[128,1536]{1,0:T(8,128)(2,1)}, u32[]{:S(2)}, u32[]{:S(2)}) collective-permute-start(f16[128,1536]{1,0:T(8,128)(2,1)} %fusion.3), channel_id=1, source_target_pairs={{0,32},{1,225},{32,64},{33,1},{64,96},{65,33},{96,128},{97,65},{12... | collective-permute-start | bytes 1179656 | tf_op jit(solution)/shard_map/ppermute | solution.py:242
  70.7 16.3 %collective-permute-start.5 = (f16[256,1536]{1,0:T(8,128)(2,1)}, f16[256,1536]{1,0:T(8,128)(2,1)}, u32[]{:S(2)}, u32[]{:S(2)}) collective-permute-start(f16[256,1536]{1,0:T(8,128)(2,1)} %fusion), channel_id=1, source_target_pairs={{0,32},{1,225},{32,64},{33,1},{64,96},{65,33},{96,128},{97,65},{12... | collective-permute-start | bytes 2359304 | tf_op jit(solution)/shard_map/ppermute | solution.py:242
  72.6 23.6 %all-to-all-start.2 = ((bf16[32,32,512]{2,1,0:T(8,128)(2,1)}), bf16[32,32,512]{2,1,0:T(8,128)(2,1)}, u32[]{:S(2)}, u32[]{:S(2)}) async-start(bf16[32,32,512]{2,1,0:T(8,128)(2,1)} %bitcast.22), calls=%async_computation.2 | async-start | bytes 2097152 | tf_op jit(solution)/shard_map/all_to_all | solution.py:229
  83.9 15.4 %collective-permute-start.7 = (f16[256,1536]{1,0:T(8,128)(2,1)}, f16[256,1536]{1,0:T(8,128)(2,1)}, u32[]{:S(2)}, u32[]{:S(2)}) collective-permute-start(f16[256,1536]{1,0:T(8,128)(2,1)} %add_convert_fusion.1), channel_id=1, source_target_pairs={{0,32},{1,225},{32,64},{33,1},{64,96},{65,33},{96,128},{97,65},{12... | collective-permute-start | bytes 2359304 | tf_op jit(solution)/shard_map/ppermute | solution.py:242
  89.2 16.1 %collective-permute-start.6 = (f16[256,1536]{1,0:T(8,128)(2,1)}, f16[256,1536]{1,0:T(8,128)(2,1)}, u32[]{:S(2)}, u32[]{:S(2)}) collective-permute-start(f16[256,1536]{1,0:T(8,128)(2,1)} %add_convert_fusion), channel_id=1, source_target_pairs={{0,33},{1,224},{32,65},{33,0},{64,97},{65,32},{96,129},{97,64},{12... | collective-permute-start | bytes 2359304 | tf_op jit(solution)/shard_map/ppermute | solution.py:242
  100.4 9.5 %collective-permute-start.9 = (f16[256,768]{1,0:T(8,128)(2,1)S(1)}, f16[256,768]{1,0:T(8,128)(2,1)S(1)}, u32[]{:S(2)}, u32[]{:S(2)}) collective-permute-start(f16[256,768]{1,0:T(8,128)(2,1)S(1)} %fusion.1), channel_id=1, source_target_pairs={{0,32},{1,225},{32,64},{33,1},{64,96},{65,33},{96,128},{97,65},{12... | collective-permute-start | bytes 1179656 | tf_op jit(solution)/shard_map/ppermute | solution.py:242
  102.6 7.4 %copy-start.8 = (s32[1,2,12]{2,1,0:T(2,128)S(1)}, s32[1,2,12]{2,1,0:T(2,128)}, u32[]{:S(2)}) copy-start(s32[1,2,12]{2,1,0:T(2,128)} %param.10) | copy-start | bytes 292
  102.6 11.5 %collective-permute-start.8 = (f16[256,768]{1,0:T(8,128)(2,1)S(1)}, f16[256,768]{1,0:T(8,128)(2,1)S(1)}, u32[]{:S(2)}, u32[]{:S(2)}) collective-permute-start(f16[256,768]{1,0:T(8,128)(2,1)S(1)} %fusion.2), channel_id=1, source_target_pairs={{0,32},{1,225},{32,64},{33,1},{64,96},{65,33},{96,128},{97,65},{12... | collective-permute-start | bytes 1179656 | tf_op jit(solution)/shard_map/ppermute | solution.py:242
  105.2 4.7 %copy-start.2 = (f32[1,256,1536]{2,1,0:T(8,128)S(1)}, f32[1,256,1536]{2,1,0:T(8,128)}, u32[]{:S(2)}) copy-start(f32[1,256,1536]{2,1,0:T(8,128)} %param.11) | copy-start | bytes 4718596
  105.2 4.7 %copy-start.3 = (f32[1,256,1536]{2,1,0:T(8,128)S(1)}, f32[1,256,1536]{2,1,0:T(8,128)}, u32[]{:S(2)}) copy-start(f32[1,256,1536]{2,1,0:T(8,128)} %param.12) | copy-start | bytes 4718596
  105.2 4.7 %copy-start.4 = (f32[1,256,1536]{2,1,0:T(8,128)S(1)}, f32[1,256,1536]{2,1,0:T(8,128)}, u32[]{:S(2)}) copy-start(f32[1,256,1536]{2,1,0:T(8,128)} %param.13) | copy-start | bytes 4718596
